TPU v7x, 128 devices: a whole 4x4x4 slice. The times are simulated.
128 devices in a mesh: dp: 8 (over y_hi, x), tensor: 16 (over y_lo, z, core).
Axes of the slice: x: 4, y: 4 (y_hi: 2, y_lo: 2; y = y_hi * 2 + y_lo), z: 4, core: 2. Of those that a mesh axis runs over, the one named last changes fastest.
Arguments:
- inputs: bfloat16 [4096, 4096], P(('dp', 'tensor')), may hold values from -6 to 6
- out_grads: bfloat16 [4096, 4096], P(('dp', 'tensor')), may hold values from -6 to 6
- w_gate: bfloat16 [4096, 14784], P(None, 'tensor'), may hold values from -0.09375 to 0.09375
- w_up: bfloat16 [4096, 14784], P(None, 'tensor'), may hold values from -0.09375 to 0.09375
- w_down: bfloat16 [14784, 4096], P('tensor'), may hold values from -0.046875 to 0.046875
Outputs:
- in_grads: bfloat16 [4096, 4096], P(('dp', 'tensor'))
- g_gate: bfloat16 [4096, 14784], P('dp', 'tensor')
- g_up: bfloat16 [4096, 14784], P('dp', 'tensor')
- g_down: bfloat16 [14784, 4096], P('tensor', 'dp')
All inputs are finite; a program needn't handle non-finite values.
Results may differ from a plain program's by a relative error of at most 0.023.
Values may be sent and summed in bfloat16 or wider, within the bound.
No kernel may reach another device: no remote copies, remote signals or barrier semaphores. Data moves between devices by JAX's collectives and lax.ppermute only.
A program may use at most 192 MiB of HBM per device.

v0:
```python
import functools

import jax
import jax.numpy as jnp
from jax import lax
from jax.experimental import pallas as pl
from jax.experimental.pallas import tpu as pltpu
from jax.sharding import Mesh, PartitionSpec as P

D = 4096
FF = 924
TILE = 256
N_TILES = 4
LAST = 160
ROWS = 3 * (3 * TILE + LAST)
BF = jnp.bfloat16
F32 = jnp.float32
VMEM_LIMIT = 48 * 1024 * 1024
ANY = pl.BlockSpec(memory_space=pl.ANY)
COST = 8


ORDER = (((0, 0), (0, 1), (0, 3), (1, 0)), ((0, 2), (1, 2), (1, 1), (1, 3)))
SLOT = {step: (b, k) for b in range(2) for k, step in enumerate(ORDER[b])}


def ring(n, step):
    return [(i, (i + step) % n) for i in range(n)]


def send_x(a, step):
    return lax.ppermute(a, "x", ring(4, step))


def send_z(a, step):
    return lax.ppermute(a, "z", ring(4, step))


def swap(a, axis):
    return lax.ppermute(a, axis, [(0, 1), (1, 0)])


def dot(a, b, ca, cb):
    return lax.dot_general(a, b, (((ca,), (cb,)), ((), ())), preferred_element_type=F32)


def after(a, *others):
    return lax.optimization_barrier((a, *others))[0]


def hidden_kernel(places, *refs):
    pieces, (wg_ref, wu_ref, wd_ref, dt_ref, dn_ref, tok, sems) = refs[:-7], refs[-7:]
    j = pl.program_id(0)

    @pl.when(j == 0)
    def _():
        copies = []

        def put(src, dst):
            copies.append(pltpu.make_async_copy(src, dst, sems.at[len(copies)]))

        for c in range(2):
            for i, place in enumerate(places):
                ref = pieces[len(places) * c + i]
                for part, (array, k) in enumerate(place):
                    dst = pl.ds(128 * c + 32 * k, 32)
                    if array is None:
                        put(ref, tok.at[:, dst, :])
                    else:
                        put(ref.at[part], tok.at[array, dst, :])
        for copy in copies:
            copy.start()
        for copy in copies:
            copy.wait()

    gate = dot(wg_ref[...], tok[0], 1, 1)
    up = dot(wu_ref[...], tok[0], 1, 1)
    d_hidden = dot(wd_ref[...], tok[1], 1, 1)
    sig = 1.0 / (1.0 + jnp.exp(-gate))
    act = gate * sig
    hidden = (act * up).astype(BF)
    d_up = (d_hidden * act).astype(BF)
    d_gate = (d_hidden * up * sig * (1.0 + gate * (1.0 - sig))).astype(BF)
    dn_ref[0] = d_gate.T
    dn_ref[1] = d_up.T

    @pl.when(j < N_TILES - 1)
    def _():
        dt_ref[:TILE] = d_gate
        dt_ref[TILE : 2 * TILE] = d_up
        dt_ref[2 * TILE :] = hidden

    @pl.when(j == N_TILES - 1)
    def _():
        dt_ref[:LAST] = d_gate[:LAST]
        dt_ref[LAST : 2 * LAST] = d_up[:LAST]
        dt_ref[2 * LAST : 3 * LAST] = hidden[:LAST]


def hidden_call(pieces, places, wg_rows, wu_rows, w_down):
    weight = pl.BlockSpec((TILE, D), lambda j: (j, 0))
    return pl.pallas_call(
        functools.partial(hidden_kernel, places),
        grid=(N_TILES,),
        in_specs=[ANY] * len(pieces) + [weight] * 3,
        out_specs=[
            pl.BlockSpec((3 * TILE, 256), lambda j: (j, 0)),
            pl.BlockSpec((2, 256, TILE), lambda j: (0, 0, j)),
        ],
        out_shape=[
            jax.ShapeDtypeStruct((ROWS, 256), BF),
            jax.ShapeDtypeStruct((2, 256, FF), BF),
        ],
        scratch_shapes=[pltpu.VMEM((2, 256, D), BF), pltpu.SemaphoreType.DMA((16,))],
        compiler_params=pltpu.CompilerParams(vmem_limit_bytes=VMEM_LIMIT),
        cost_estimate=pl.CostEstimate(
            flops=6 * 256 * D * FF // COST, bytes_accessed=6 * D * FF // COST, transcendentals=0
        ),
        name="hidden_grads",
    )(*pieces, wg_rows, wu_rows, w_down)


def in_grads_kernel(pos_ref, dn0_ref, dn1_ref, wg_ref, wu_ref, own_ref, other_ref, dn):
    @pl.when(pl.program_id(0) == 0)
    def _():
        for a in range(2):
            dn[a, :256, :] = dn0_ref[a]
            dn[a, 256:, :] = dn1_ref[a]

    p = (dot(dn[0], wg_ref[...], 1, 0) + dot(dn[1], wu_ref[...], 1, 0)).astype(BF)
    yl, z = pos_ref[0], pos_ref[1]
    for b in range(2):
        for c, out_ref in enumerate((own_ref, other_ref)):
            for i, (y_step, z_step) in enumerate(ORDER[b]):
                row = 256 * b + 128 * c + 32 * i
                out_ref[y_step ^ yl, lax.rem(z_step + z, 4)] = p[row : row + 32]


def in_grads_call(pos, dn0, dn1, wg_rows, wu_rows):
    cols = 512
    whole = pl.BlockSpec((2, 256, FF), lambda j, p: (0, 0, 0))
    weight = pl.BlockSpec((FF, cols), lambda j, p: (0, j))
    out = pl.BlockSpec((2, 4, 32, cols), lambda j, p: (0, 0, 0, j))
    return pl.pallas_call(
        in_grads_kernel,
        grid_spec=pltpu.PrefetchScalarGridSpec(
            num_scalar_prefetch=1,
            grid=(D // cols,),
            in_specs=[whole, whole, weight, weight],
            out_specs=[out, out],
            scratch_shapes=[pltpu.VMEM((2, 512, FF), BF)],
        ),
        out_shape=[jax.ShapeDtypeStruct((2, 4, 32, D), BF)] * 2,
        compiler_params=pltpu.CompilerParams(vmem_limit_bytes=VMEM_LIMIT),
        cost_estimate=pl.CostEstimate(
            flops=4 * 512 * D * FF // COST, bytes_accessed=4 * D * FF // COST, transcendentals=0
        ),
        name="in_grads_terms",
    )(pos, dn0, dn1, wg_rows, wu_rows)


def weights_kernel(n, starts, *refs):
    pieces, col_pieces = refs[:8], refs[8:18]
    send_ref, keep_ref, stack, x, sems = refs[18:]
    halves = ([], [])
    count = [0]

    def put(group, src, dst):
        copy = pltpu.make_async_copy(src, dst, sems.at[count[0]])
        count[0] += 1
        copy.start()
        group.append(copy)

    for b in range(2):
        for s in range(4):
            i = 4 * b + s
            put(
                halves[0],
                pieces[i].at[pl.ds(starts[i], 3 * n), :],
                stack.at[b, :, pl.ds(256 * s, 256)],
            )
    for h in range(2):
        cols = pl.ds(512 * h, 512)
        for c in range(2):
            here, left, far_in, far_grad, right = col_pieces[5 * c : 5 * c + 5]
            for y in range(2):
                for z, ref in ((0, here), (1, left), (3, right)):
                    b, k = SLOT[y, z]
                    put(halves[h], ref.at[y, :, :, :, cols], x.at[b, :, :, c, k, :, cols])
                b, k = SLOT[y, 2]
                put(halves[h], far_in.at[y, :, :, cols], x.at[b, 0, :, c, k, :, cols])
                put(halves[h], far_grad.at[y, :, :, cols], x.at[b, 1, :, c, k, :, cols])

    for h, out_ref in enumerate((send_ref, keep_ref)):
        for copy in halves[h]:
            copy.wait()

        def total(rows, a):
            parts = [
                dot(stack[b, rows, :], x[b, a, :, :, :, :, 512 * h : 512 * h + 512].reshape(1024, 512), 1, 0)
                for b in range(2)
            ]
            return (parts[0] + parts[1]).astype(BF)

        out_ref[: 2 * n] = total(slice(0, 2 * n), 0)
        out_ref[2 * n :] = total(slice(2 * n, 3 * n), 1)


def weights_call(n, pieces, col_pieces):
    return pl.pallas_call(
        functools.partial(weights_kernel, n, [s for _, s in pieces]),
        in_specs=[ANY] * 18,
        out_specs=[pl.BlockSpec(memory_space=pltpu.VMEM)] * 2,
        out_shape=[jax.ShapeDtypeStruct((3 * n, 512), BF)] * 2,
        scratch_shapes=[
            pltpu.VMEM((2, 3 * n, 1024), BF),
            pltpu.VMEM((2, 2, 4, 2, 4, 32, 1024), BF),
            pltpu.SemaphoreType.DMA((48,)),
        ],
        compiler_params=pltpu.CompilerParams(vmem_limit_bytes=VMEM_LIMIT),
        cost_estimate=pl.CostEstimate(
            flops=6 * n * 2048 * 1024 // COST, bytes_accessed=(12 << 20) // COST, transcendentals=0
        ),
        name="weight_grads",
    )(*[a for a, _ in pieces], *col_pieces)


def gate(*arrays):
    return lax.optimization_barrier(arrays)


def core_swaps(pieces):
    return [swap(p, "core") for p in pieces]


def on_device(inputs, out_grads, w_gate, w_up, w_down):
    xi, yh, yl, zi = (lax.axis_index(a) for a in ("x", "yh", "yl", "z"))
    pos = jnp.stack([yl, zi]).astype(jnp.int32)
    wg_rows, wu_rows = w_gate.T, w_up.T
    mine = jnp.stack([inputs, out_grads])

    def block_for(step):
        group = lax.rem(xi + step, 4)
        starts = [((1 - yh) * 4 + group) * 512, (yh * 4 + group) * 512]
        return jnp.concatenate([lax.dynamic_slice_in_dim(mine, s, 512, axis=2) for s in starts], axis=2)

    right, left = send_z(mine, 1), send_z(mine, -1)
    partner = swap(mine, "yl")
    from_x = [block_for(0), send_x(block_for(1), 1), send_x(block_for(3), -1), send_x(block_for(2), 2)]
    right, left, partner, *from_x = gate(right, left, partner, *from_x)

    shares = jnp.stack(from_x, axis=1)
    other_shares = swap(shares, "yl")
    p_right, p_left = send_z(partner, 1), send_z(partner, -1)
    batch0 = [mine, left, right, partner]
    batch0 += core_swaps(batch0)
    both = ((None, 0),), ((None, 1),), ((None, 2),), ((None, 3),)
    dt0, dn0 = hidden_call(batch0, both, wg_rows, wu_rows, w_down)
    dt0, dn0, p_right, p_left, shares, other_shares = gate(dt0, dn0, p_right, p_left, shares, other_shares)

    lanes = {1: [], -1: []}

    def in_turn(a, step):
        lane = lanes[step]
        if len(lane) >= 2:
            a = after(a, lane[-2])
        lane.append(send_x(a, step))
        return lane[-1]

    right0, left0 = in_turn(dt0, 1), in_turn(dt0, -1)
    far_in = send_z(jnp.stack([right[0], p_right[0]]), 1)
    far_grad = send_z(jnp.stack([left[1], p_left[1]]), -1)
    batch1 = [far_in, far_grad, p_left, p_right]
    batch1 += core_swaps(batch1)
    shares = jnp.stack([shares, other_shares])
    shares, *batch1 = gate(shares, *batch1)

    places = ((0, 0), (0, 1)), ((1, 0), (1, 1)), ((None, 2),), ((None, 3),)
    dt1, dn1 = hidden_call(batch1, places, wg_rows, wu_rows, w_down)
    c_right, c_left = send_z(shares, 1), send_z(shares, -1)
    dt1, dn1, c_right, c_left, right0, left0 = gate(dt1, dn1, c_right, c_left, right0, left0)

    term_own, term_other = in_grads_call(pos, dn0, dn1, wg_rows, wu_rows)
    col_pieces = [shares, c_left, send_z(c_right[:, 0], 1), send_z(c_left[:, 1], -1), c_right]
    col_pieces += core_swaps(col_pieces)

    kept, sent = [], []
    for j in range(N_TILES):
        n = TILE if j < N_TILES - 1 else LAST
        start = 3 * TILE * j
        rows = slice(start, start + 3 * n)
        right0_rows, dt1_rows = right0[rows], dt1[rows]
        if j == 1:
            term_own, term_other, right0_rows, dt1_rows = gate(term_own, term_other, right0_rows, dt1_rows)
        if j >= 2:
            send, keep, right0_rows, dt1_rows = gate(sent[j - 2], kept[j - 2], right0_rows, dt1_rows)
            sent[j - 2], kept[j - 2] = send, keep
        far0, left1 = in_turn(right0_rows, 1), in_turn(dt1_rows, -1)
        right1, far1 = in_turn(dt1_rows, 1), in_turn(left1, -1)
        pieces = [
            (dt0, start), (right0, start), (left0, start), (far0, 0),
            (dt1, start), (right1, 0), (left1, 0), (far1, 0),
        ]
        send, keep = weights_call(n, pieces, col_pieces)
        kept.append(keep)
        sent.append(send)

    sent = [swap(a, "yh") for a in sent]
    pair = (term_own.astype(F32) + swap(term_other, "core").astype(F32)).astype(BF)
    in_grads = lax.psum_scatter(pair.reshape(256, D), ("yl", "z"), scatter_dimension=0, tiled=True)

    gate_parts, up_parts, down_parts = [], [], []
    for j in range(N_TILES):
        n = TILE if j < N_TILES - 1 else LAST
        used = min(n, FF - TILE * j)
        total = (kept[j].astype(F32) + sent[j].astype(F32)).astype(BF)
        gate_parts.append(total[:used])
        up_parts.append(total[n : n + used])
        down_parts.append(total[2 * n : 2 * n + used])
    g_gate = jnp.concatenate(gate_parts, axis=0).T
    g_up = jnp.concatenate(up_parts, axis=0).T
    g_down = jnp.concatenate(down_parts, axis=0)
    return in_grads, g_gate, g_up, g_down


def solution(mesh):
    fine = Mesh(mesh.devices.reshape(2, 4, 2, 4, 2), ("yh", "x", "yl", "z", "core"))
    tokens = P(("yh", "x", "yl", "z", "core"), None)
    units = ("yl", "z", "core")
    groups = ("yh", "x")
    return jax.shard_map(
        on_device,
        mesh=fine,
        in_specs=(tokens, tokens, P(None, units), P(None, units), P(units, None)),
        out_specs=(tokens, P(groups, units), P(groups, units), P(units, groups)),
        check_vma=False,
    )
```

profile of v0, /device:TPU:0, one launch (start us, length us, event | category | flops | bytes accessed | tf_op | source)
XLA Modules:
  0.0 241.5 jit_solution(11415982429269244152)
XLA Ops:
  23.4 4.5 %collective-permute-done.5 = bf16[2,32,1024]{2,1,0:T(8,128)(2,1)S(1)} collective-permute-done((bf16[2,32,1024]{2,1,0:T(8,128)(2,1)S(1)}, bf16[2,32,1024]{2,1,0:T(8,128)(2,1)S(1)}, u32[]{:S(2)}, u32[]{:S(2)}) %collective-permute-start.5) | collective-permute-done | bytes 131104 | tf_op jit(solution)/shard_map/ppermute | solution.py:32
  28.7 3.2 %collective-permute-start.11 = (bf16[2,32,4096]{2,1,0:T(8,128)(2,1)S(1)}, bf16[2,32,4096]{2,1,0:T(8,128)(2,1)S(1)}, u32[]{:S(2)}, u32[]{:S(2)}) collective-permute-start(bf16[2,32,4096]{2,1,0:T(8,128)(2,1)S(1)} %collective-permute-done.2.refs_3_), channel_id=1, source_target_pairs={{0,6},{2,0},{4,2},{6,4},{1,7},{3,1},{5,3},{7,5},{8,14},{10,8},{12,... | collective-permute-start | bytes 1572872 | tf_op jit(solution)/shard_map/ppermute | solution.py:36
  32.4 12.9 %hidden_grads.2 = (bf16[2784,256]{1,0:T(8,128)(2,1)}, bf16[2,256,924]{2,1,0:T(8,128)(2,1)S(1)}) custom-call(bf16[2,32,4096]{2,1,0:T(8,128)(2,1)S(1)} %pad_maximum_fusion.refs_0_, bf16[2,32,4096]{2,1,0:T(8,128)(2,1)S(1)} %collective-permute-done.1.refs_1_, bf16[2,32,4096]{2,1,0:T(8,128)(2,1)S(1)} %collective-permute-done.refs_2_, ...), custom_call_target="tpu_custom_call" | custom-call | flops 726663168 | bytes 2838528 | tf_op jit(solution)/shard_map/hidden_grads/pallas_call | solution.py:102
  46.2 3.3 %collective-permute-start.14 = (bf16[2,32,4096]{2,1,0:T(8,128)(2,1)S(1)}, bf16[2,32,4096]{2,1,0:T(8,128)(2,1)S(1)}, u32[]{:S(2)}, u32[]{:S(2)}) collective-permute-start(bf16[2,32,4096]{2,1,0:T(8,128)(2,1)S(1)} %pad_maximum_fusion.5), channel_id=1, source_target_pairs={{0,6},{2,0},{4,2},{6,4},{1,7},{3,1},{5,3},{7,5},{8,14},{10,8},{12,... | collective-permute-start | bytes 1572872 | tf_op jit(solution)/shard_map/ppermute | solution.py:36
  50.0 10.6 %collective-permute-done.13.refs_0_ = bf16[2,32,4096]{2,1,0:T(8,128)(2,1)S(1)} collective-permute-done((bf16[2,32,4096]{2,1,0:T(8,128)(2,1)S(1)}, bf16[2,32,4096]{2,1,0:T(8,128)(2,1)S(1)}, u32[]{:S(2)}, u32[]{:S(2)}) %collective-permute-start.13) | collective-permute-done | bytes 524320 | tf_op jit(solution)/shard_map/ppermute | solution.py:36
  66.9 3.2 %collective-permute-start.20 = (bf16[2,2,4,32,1024]{4,3,2,1,0:T(8,128)(2,1)S(1)}, bf16[2,2,4,32,1024]{4,3,2,1,0:T(8,128)(2,1)S(1)}, u32[]{:S(2)}, u32[]{:S(2)}) collective-permute-start(bf16[2,2,4,32,1024]{4,3,2,1,0:T(8,128)(2,1)S(1)} %pad_maximum_fusion.1.refs_8_), channel_id=1, source_target_pairs={{0,6},{2,0},{4,2},{6,4},{1,7},{3,1},{5,3},{7,5},{8,14},{10,8},{12,... | collective-permute-start | bytes 3145736 | tf_op jit(solution)/shard_map/ppermute | solution.py:36
  76.5 12.9 %hidden_grads.3 = (bf16[2784,256]{1,0:T(8,128)(2,1)}, bf16[2,256,924]{2,1,0:T(8,128)(2,1)S(1)}) custom-call(bf16[2,32,4096]{2,1,0:T(8,128)(2,1)S(1)} %copy-done.7, bf16[2,32,4096]{2,1,0:T(8,128)(2,1)S(1)} %copy-done.9, bf16[2,32,4096]{2,1,0:T(8,128)(2,1)S(1)} %collective-permute-done.11.refs_2_, bf16[2,32,4096]{2,1,0:T(8,128)(2,1)S(1)} %collective-permute-done.10.refs_3_, ...), custom_call_target="tpu_custom_call" | custom-call | flops 726663168 | bytes 2838528 | tf_op jit(solution)/shard_map/hidden_grads/pallas_call | solution.py:102
  89.4 6.4 %collective-permute-done.21.refs_1_ = bf16[2784,256]{1,0:T(8,128)(2,1)} collective-permute-done((bf16[2784,256]{1,0:T(8,128)(2,1)}, bf16[2784,256]{1,0:T(8,128)(2,1)}, u32[]{:S(2)}, u32[]{:S(2)}) %collective-permute-start.21) | collective-permute-done | bytes 1425440 | tf_op jit(solution)/shard_map/ppermute | solution.py:32
  99.6 14.1 %in_grads_terms.1 = (bf16[2,4,32,4096]{3,2,1,0:T(8,128)(2,1)S(1)}, bf16[2,4,32,4096]{3,2,1,0:T(8,128)(2,1)}) custom-call(s32[2]{0:T(128)S(1)} %pad_add_fusion.pos_ref, bf16[2,256,924]{2,1,0:T(8,128)(2,1)S(1)} %copy-done.5, bf16[2,256,924]{2,1,0:T(8,128)(2,1)S(1)} %get-tuple-element.98.dn1_ref, bf16[924,4096]{1,0:T(8,128)(2,1)} %bitcast.29, ...), custom_call_target="tpu_custom_call" | custom-call | flops 968884224 | bytes 1892352 | tf_op jit(solution)/shard_map/in_grads_terms/pallas_call | solution.py:144
  120.7 5.8 %collective-permute-done.24.refs_3_ = bf16[768,256]{1,0:T(8,128)(2,1)S(1)} collective-permute-done((bf16[768,256]{1,0:T(8,128)(2,1)S(1)}, bf16[768,256]{1,0:T(8,128)(2,1)S(1)}, u32[]{:S(2)}, u32[]{:S(2)}) %collective-permute-start.24) | collective-permute-done | bytes 393248 | tf_op jit(solution)/shard_map/ppermute | solution.py:32
  131.9 6.3 %collective-permute-done.25.refs_5_ = bf16[768,256]{1,0:T(8,128)(2,1)S(1)} collective-permute-done((bf16[768,256]{1,0:T(8,128)(2,1)}, bf16[768,256]{1,0:T(8,128)(2,1)S(1)}, u32[]{:S(2)}, u32[]{:S(2)}) %collective-permute-start.25) | collective-permute-done | bytes 393248 | tf_op jit(solution)/shard_map/ppermute | solution.py:32
  141.6 6.0 %collective-permute-done.27.refs_7_ = bf16[768,256]{1,0:T(8,128)(2,1)S(1)} collective-permute-done((bf16[768,256]{1,0:T(8,128)(2,1)S(1)}, bf16[768,256]{1,0:T(8,128)(2,1)S(1)}, u32[]{:S(2)}, u32[]{:S(2)}) %collective-permute-start.27) | collective-permute-done | bytes 393248 | tf_op jit(solution)/shard_map/ppermute | solution.py:32
  149.7 6.5 %weight_grads.4 = (bf16[768,512]{1,0:T(8,128)(2,1)S(1)}, bf16[768,512]{1,0:T(8,128)(2,1)S(1)}) custom-call(bf16[2784,256]{1,0:T(8,128)(2,1)} %get-tuple-element.97.refs_0_, bf16[2784,256]{1,0:T(8,128)(2,1)} %collective-permute-done.21.refs_1_, bf16[2784,256]{1,0:T(8,128)(2,1)} %collective-permute-done.22.refs_2_, ...), custom_call_target="tpu_custom_call" | custom-call | flops 402653184 | bytes 1572864 | tf_op jit(solution)/shard_map/weight_grads/pallas_call | solution.py:210
  156.2 3.3 %collective-permute-start.35 = (bf16[768,512]{1,0:T(8,128)(2,1)S(1)}, bf16[768,512]{1,0:T(8,128)(2,1)S(1)}, u32[]{:S(2)}, u32[]{:S(2)}) collective-permute-start(bf16[768,512]{1,0:T(8,128)(2,1)S(1)} %get-tuple-element.113), channel_id=1, source_target_pairs={{0,64},{64,0},{1,65},{65,1},{2,66},{66,2},{3,67},{67,3},{4,68},{68... | collective-permute-start | bytes 2359304 | tf_op jit(solution)/shard_map/ppermute | solution.py:40
  164.7 6.0 %collective-permute-done.37.refs_5_ = bf16[768,256]{1,0:T(8,128)(2,1)S(1)} collective-permute-done((bf16[768,256]{1,0:T(8,128)(2,1)}, bf16[768,256]{1,0:T(8,128)(2,1)S(1)}, u32[]{:S(2)}, u32[]{:S(2)}) %collective-permute-start.37) | collective-permute-done | bytes 393248 | tf_op jit(solution)/shard_map/ppermute | solution.py:32
  172.6 6.5 %weight_grads.5 = (bf16[768,512]{1,0:T(8,128)(2,1)S(1)}, bf16[768,512]{1,0:T(8,128)(2,1)S(1)}) custom-call(bf16[2784,256]{1,0:T(8,128)(2,1)} %get-tuple-element.97.refs_0_, bf16[2784,256]{1,0:T(8,128)(2,1)} %collective-permute-done.21.refs_1_, bf16[2784,256]{1,0:T(8,128)(2,1)} %collective-permute-done.22.refs_2_, ...), custom_call_target="tpu_custom_call" | custom-call | flops 402653184 | bytes 1572864 | tf_op jit(solution)/shard_map/weight_grads/pallas_call | solution.py:210
  179.1 3.8 %collective-permute-start.40 = (bf16[768,512]{1,0:T(8,128)(2,1)S(1)}, bf16[768,512]{1,0:T(8,128)(2,1)S(1)}, u32[]{:S(2)}, u32[]{:S(2)}) collective-permute-start(bf16[768,512]{1,0:T(8,128)(2,1)S(1)} %get-tuple-element.123), channel_id=1, source_target_pairs={{0,64},{64,0},{1,65},{65,1},{2,66},{66,2},{3,67},{67,3},{4,68},{68... | collective-permute-start | bytes 2359304 | tf_op jit(solution)/shard_map/ppermute | solution.py:40
  182.9 3.2 %collective-permute-start.44 = (bf16[768,256]{1,0:T(8,128)(2,1)S(1)}, bf16[768,256]{1,0:T(8,128)(2,1)S(1)}, u32[]{:S(2)}, u32[]{:S(2)}) collective-permute-start(bf16[768,256]{1,0:T(8,128)(2,1)S(1)} %collective-permute-done.43.refs_6_), channel_id=1, source_target_pairs={{0,48},{16,0},{32,16},{48,32},{1,49},{17,1},{33,17},{49,33},{2,50}... | collective-permute-start | bytes 1179656 | tf_op jit(solution)/shard_map/ppermute | solution.py:32
  186.8 3.2 %collective-permute-start.48 = (bf16[480,256]{1,0:T(8,128)(2,1)S(1)}, bf16[480,256]{1,0:T(8,128)(2,1)S(1)}, u32[]{:S(2)}, u32[]{:S(2)}) collective-permute-start(bf16[480,256]{1,0:T(8,128)(2,1)S(1)} %slice.92), channel_id=1, source_target_pairs={{0,48},{16,0},{32,16},{48,32},{1,49},{17,1},{33,17},{49,33},{2,50}... | collective-permute-start | bytes 737288 | tf_op jit(solution)/shard_map/ppermute | solution.py:32
  190.2 7.1 %collective-permute-done.48.refs_6_ = bf16[480,256]{1,0:T(8,128)(2,1)S(1)} collective-permute-done((bf16[480,256]{1,0:T(8,128)(2,1)S(1)}, bf16[480,256]{1,0:T(8,128)(2,1)S(1)}, u32[]{:S(2)}, u32[]{:S(2)}) %collective-permute-start.48) | collective-permute-done | bytes 245792 | tf_op jit(solution)/shard_map/ppermute | solution.py:32
  197.3 3.3 %collective-permute-start.49 = (bf16[480,256]{1,0:T(8,128)(2,1)S(1)}, bf16[480,256]{1,0:T(8,128)(2,1)S(1)}, u32[]{:S(2)}, u32[]{:S(2)}) collective-permute-start(bf16[480,256]{1,0:T(8,128)(2,1)S(1)} %collective-permute-done.48.refs_6_), channel_id=1, source_target_pairs={{0,48},{16,0},{32,16},{48,32},{1,49},{17,1},{33,17},{49,33},{2,50}... | collective-permute-start | bytes 737288 | tf_op jit(solution)/shard_map/ppermute | solution.py:32
  200.7 6.6 %weight_grads.6 = (bf16[768,512]{1,0:T(8,128)(2,1)S(1)}, bf16[768,512]{1,0:T(8,128)(2,1)S(1)}) custom-call(bf16[2784,256]{1,0:T(8,128)(2,1)} %get-tuple-element.97.refs_0_, bf16[2784,256]{1,0:T(8,128)(2,1)} %collective-permute-done.21.refs_1_, bf16[2784,256]{1,0:T(8,128)(2,1)} %collective-permute-done.22.refs_2_, ...), custom_call_target="tpu_custom_call" | custom-call | flops 402653184 | bytes 1572864 | tf_op jit(solution)/shard_map/weight_grads/pallas_call | solution.py:210
  210.0 4.9 %weight_grads.7 = (bf16[480,512]{1,0:T(8,128)(2,1)S(1)}, bf16[480,512]{1,0:T(8,128)(2,1)S(1)}) custom-call(bf16[2784,256]{1,0:T(8,128)(2,1)} %get-tuple-element.97.refs_0_, bf16[2784,256]{1,0:T(8,128)(2,1)} %collective-permute-done.21.refs_1_, bf16[2784,256]{1,0:T(8,128)(2,1)} %collective-permute-done.22.refs_2_, ...), custom_call_target="tpu_custom_call" | custom-call | flops 251658240 | bytes 1572864 | tf_op jit(solution)/shard_map/weight_grads/pallas_call | solution.py:210
  216.2 15.7 %collective-permute-done.50 = bf16[480,512]{1,0:T(8,128)(2,1)S(1)} collective-permute-done((bf16[480,512]{1,0:T(8,128)(2,1)S(1)}, bf16[480,512]{1,0:T(8,128)(2,1)S(1)}, u32[]{:S(2)}, u32[]{:S(2)}) %collective-permute-start.50) | collective-permute-done | bytes 491552 | tf_op jit(solution)/shard_map/ppermute | solution.py:40
  (169 shorter events, 67.7 us)
Async XLA Ops:
  7.2 227.5 %reduce-scatter.2.cloned.1.call-start = ((), (), s32[]{:S(2)}) async-start(), calls=%async_computation.1 | async-start | bytes 2359296 | tf_op jit(solution)/shard_map/reduce_scatter | solution.py:310
  8.4 19.6 %collective-permute-start = (bf16[2,32,4096]{2,1,0:T(8,128)(2,1)S(1)}, bf16[2,32,4096]{2,1,0:T(8,128)(2,1)S(1)}, u32[]{:S(2)}, u32[]{:S(2)}) collective-permute-start(bf16[2,32,4096]{2,1,0:T(8,128)(2,1)S(1)} %pad_maximum_fusion.refs_0_), channel_id=1, source_target_pairs={{0,2},{2,4},{4,6},{6,0},{1,3},{3,5},{5,7},{7,1},{8,10},{10,12},{12... | collective-permute-start | bytes 1572872 | tf_op jit(solution)/shard_map/ppermute | solution.py:36
  10.4 17.5 %collective-permute-start.1 = (bf16[2,32,4096]{2,1,0:T(8,128)(2,1)S(1)}, bf16[2,32,4096]{2,1,0:T(8,128)(2,1)S(1)}, u32[]{:S(2)}, u32[]{:S(2)}) collective-permute-start(bf16[2,32,4096]{2,1,0:T(8,128)(2,1)S(1)} %pad_maximum_fusion.refs_0_), channel_id=1, source_target_pairs={{0,6},{2,0},{4,2},{6,4},{1,7},{3,1},{5,3},{7,5},{8,14},{10,8},{12,... | collective-permute-start | bytes 1572872 | tf_op jit(solution)/shard_map/ppermute | solution.py:36
  12.6 15.3 %collective-permute-start.2 = (bf16[2,32,4096]{2,1,0:T(8,128)(2,1)S(1)}, bf16[2,32,4096]{2,1,0:T(8,128)(2,1)S(1)}, u32[]{:S(2)}, u32[]{:S(2)}) collective-permute-start(bf16[2,32,4096]{2,1,0:T(8,128)(2,1)S(1)} %pad_maximum_fusion.refs_0_), channel_id=1, source_target_pairs={{0,8},{8,0},{1,9},{9,1},{2,10},{10,2},{3,11},{11,3},{4,12},{12,4},... | collective-permute-start | bytes 1572872 | tf_op jit(solution)/shard_map/ppermute | solution.py:40
  28.5 16.9 %collective-permute-start.10 = (bf16[2,32,4096]{2,1,0:T(8,128)(2,1)S(1)}, bf16[2,32,4096]{2,1,0:T(8,128)(2,1)S(1)}, u32[]{:S(2)}, u32[]{:S(2)}) collective-permute-start(bf16[2,32,4096]{2,1,0:T(8,128)(2,1)S(1)} %collective-permute-done.2.refs_3_), channel_id=1, source_target_pairs={{0,2},{2,4},{4,6},{6,0},{1,3},{3,5},{5,7},{7,1},{8,10},{10,12},{12... | collective-permute-start | bytes 1572872 | tf_op jit(solution)/shard_map/ppermute | solution.py:36
  28.7 16.7 %collective-permute-start.11 = (bf16[2,32,4096]{2,1,0:T(8,128)(2,1)S(1)}, bf16[2,32,4096]{2,1,0:T(8,128)(2,1)S(1)}, u32[]{:S(2)}, u32[]{:S(2)}) collective-permute-start(bf16[2,32,4096]{2,1,0:T(8,128)(2,1)S(1)} %collective-permute-done.2.refs_3_), channel_id=1, source_target_pairs={{0,6},{2,0},{4,2},{6,4},{1,7},{3,1},{5,3},{7,5},{8,14},{10,8},{12,... | collective-permute-start | bytes 1572872 | tf_op jit(solution)/shard_map/ppermute | solution.py:36
  49.5 14.9 %collective-permute-start.18 = (bf16[2,32,4096]{2,1,0:T(8,128)(2,1)S(1)}, bf16[2,32,4096]{2,1,0:T(8,128)(2,1)S(1)}, u32[]{:S(2)}, u32[]{:S(2)}) collective-permute-start(bf16[2,32,4096]{2,1,0:T(8,128)(2,1)S(1)} %collective-permute-done.10.refs_3_), channel_id=1, source_target_pairs={{0,1},{1,0},{2,3},{3,2},{4,5},{5,4},{6,7},{7,6},{8,9},{9,8},{10,11... | collective-permute-start | bytes 1572872 | tf_op jit(solution)/shard_map/ppermute | solution.py:40
  61.1 34.8 %collective-permute-start.21 = (bf16[2784,256]{1,0:T(8,128)(2,1)}, bf16[2784,256]{1,0:T(8,128)(2,1)}, u32[]{:S(2)}, u32[]{:S(2)}) collective-permute-start(bf16[2784,256]{1,0:T(8,128)(2,1)} %get-tuple-element.97.refs_0_), channel_id=1, source_target_pairs={{0,16},{16,32},{32,48},{48,0},{1,17},{17,33},{33,49},{49,1},{2,18}... | collective-permute-start | bytes 4276232 | tf_op jit(solution)/shard_map/ppermute | solution.py:32
  61.7 34.2 %collective-permute-start.22 = (bf16[2784,256]{1,0:T(8,128)(2,1)}, bf16[2784,256]{1,0:T(8,128)(2,1)}, u32[]{:S(2)}, u32[]{:S(2)}) collective-permute-start(bf16[2784,256]{1,0:T(8,128)(2,1)} %get-tuple-element.97.refs_0_), channel_id=1, source_target_pairs={{0,48},{16,0},{32,16},{48,32},{1,49},{17,1},{33,17},{49,33},{2,50}... | collective-permute-start | bytes 4276232 | tf_op jit(solution)/shard_map/ppermute | solution.py:32
  66.9 28.9 %collective-permute-start.19 = (bf16[2,2,4,32,1024]{4,3,2,1,0:T(8,128)(2,1)S(1)}, bf16[2,2,4,32,1024]{4,3,2,1,0:T(8,128)(2,1)}, u32[]{:S(2)}, u32[]{:S(2)}) collective-permute-start(bf16[2,2,4,32,1024]{4,3,2,1,0:T(8,128)(2,1)S(1)} %pad_maximum_fusion.1.refs_8_), channel_id=1, source_target_pairs={{0,2},{2,4},{4,6},{6,0},{1,3},{3,5},{5,7},{7,1},{8,10},{10,12},{12... | collective-permute-start | bytes 3145736 | tf_op jit(solution)/shard_map/ppermute | solution.py:36
  66.9 28.9 %collective-permute-start.20 = (bf16[2,2,4,32,1024]{4,3,2,1,0:T(8,128)(2,1)S(1)}, bf16[2,2,4,32,1024]{4,3,2,1,0:T(8,128)(2,1)S(1)}, u32[]{:S(2)}, u32[]{:S(2)}) collective-permute-start(bf16[2,2,4,32,1024]{4,3,2,1,0:T(8,128)(2,1)S(1)} %pad_maximum_fusion.1.refs_8_), channel_id=1, source_target_pairs={{0,6},{2,0},{4,2},{6,4},{1,7},{3,1},{5,3},{7,5},{8,14},{10,8},{12,... | collective-permute-start | bytes 3145736 | tf_op jit(solution)/shard_map/ppermute | solution.py:36
  117.5 32.2 %collective-permute-start.31 = (bf16[2,2,4,32,1024]{4,3,2,1,0:T(8,128)(2,1)S(1)}, bf16[2,2,4,32,1024]{4,3,2,1,0:T(8,128)(2,1)}, u32[]{:S(2)}, u32[]{:S(2)}) collective-permute-start(bf16[2,2,4,32,1024]{4,3,2,1,0:T(8,128)(2,1)S(1)} %collective-permute-done.20.refs_9_), channel_id=1, source_target_pairs={{0,1},{1,0},{2,3},{3,2},{4,5},{5,4},{6,7},{7,6},{8,9},{9,8},{10,11... | collective-permute-start | bytes 3145736 | tf_op jit(solution)/shard_map/ppermute | solution.py:40
  120.2 29.5 %collective-permute-start.34 = (bf16[2,2,4,32,1024]{4,3,2,1,0:T(8,128)(2,1)}, bf16[2,2,4,32,1024]{4,3,2,1,0:T(8,128)(2,1)}, u32[]{:S(2)}, u32[]{:S(2)}) collective-permute-start(bf16[2,2,4,32,1024]{4,3,2,1,0:T(8,128)(2,1)} %collective-permute-done.19.refs_12_), channel_id=1, source_target_pairs={{0,1},{1,0},{2,3},{3,2},{4,5},{5,4},{6,7},{7,6},{8,9},{9,8},{10,11... | collective-permute-start | bytes 3145736 | tf_op jit(solution)/shard_map/ppermute | solution.py:40
  149.3 15.0 %collective-permute-start.36 = (bf16[768,256]{1,0:T(8,128)(2,1)}, bf16[768,256]{1,0:T(8,128)(2,1)S(1)}, u32[]{:S(2)}, u32[]{:S(2)}) collective-permute-start(bf16[768,256]{1,0:T(8,128)(2,1)} %get-tuple-element.115), channel_id=1, source_target_pairs={{0,16},{16,32},{32,48},{48,0},{1,17},{17,33},{33,49},{49,1},{2,18}... | collective-permute-start | bytes 1179656 | tf_op jit(solution)/shard_map/ppermute | solution.py:32
  149.6 21.0 %collective-permute-start.37 = (bf16[768,256]{1,0:T(8,128)(2,1)}, bf16[768,256]{1,0:T(8,128)(2,1)S(1)}, u32[]{:S(2)}, u32[]{:S(2)}) collective-permute-start(bf16[768,256]{1,0:T(8,128)(2,1)} %get-tuple-element.118), channel_id=1, source_target_pairs={{0,16},{16,32},{32,48},{48,0},{1,17},{17,33},{33,49},{49,1},{2,18}... | collective-permute-start | bytes 1179656 | tf_op jit(solution)/shard_map/ppermute | solution.py:32
  156.2 30.5 %collective-permute-start.35 = (bf16[768,512]{1,0:T(8,128)(2,1)S(1)}, bf16[768,512]{1,0:T(8,128)(2,1)S(1)}, u32[]{:S(2)}, u32[]{:S(2)}) collective-permute-start(bf16[768,512]{1,0:T(8,128)(2,1)S(1)} %get-tuple-element.113), channel_id=1, source_target_pairs={{0,64},{64,0},{1,65},{65,1},{2,66},{66,2},{3,67},{67,3},{4,68},{68... | collective-permute-start | bytes 2359304 | tf_op jit(solution)/shard_map/ppermute | solution.py:40
  162.6 20.3 %collective-permute-start.43 = (bf16[768,256]{1,0:T(8,128)(2,1)S(1)}, bf16[768,256]{1,0:T(8,128)(2,1)S(1)}, u32[]{:S(2)}, u32[]{:S(2)}) collective-permute-start(bf16[768,256]{1,0:T(8,128)(2,1)S(1)} %copy-done.22), channel_id=1, source_target_pairs={{0,48},{16,0},{32,16},{48,32},{1,49},{17,1},{33,17},{49,33},{2,50}... | collective-permute-start | bytes 1179656 | tf_op jit(solution)/shard_map/ppermute | solution.py:32
  164.3 21.8 %collective-permute-start.41 = (bf16[768,256]{1,0:T(8,128)(2,1)S(1)}, bf16[768,256]{1,0:T(8,128)(2,1)S(1)}, u32[]{:S(2)}, u32[]{:S(2)}) collective-permute-start(bf16[768,256]{1,0:T(8,128)(2,1)S(1)} %copy-done.23), channel_id=1, source_target_pairs={{0,16},{16,32},{32,48},{48,0},{1,17},{17,33},{33,49},{49,1},{2,18}... | collective-permute-start | bytes 1179656 | tf_op jit(solution)/shard_map/ppermute | solution.py:32
  170.6 16.1 %collective-permute-start.42 = (bf16[768,256]{1,0:T(8,128)(2,1)S(1)}, bf16[768,256]{1,0:T(8,128)(2,1)S(1)}, u32[]{:S(2)}, u32[]{:S(2)}) collective-permute-start(bf16[768,256]{1,0:T(8,128)(2,1)S(1)} %copy-done.22), channel_id=1, source_target_pairs={{0,16},{16,32},{32,48},{48,0},{1,17},{17,33},{33,49},{49,1},{2,18}... | collective-permute-start | bytes 1179656 | tf_op jit(solution)/shard_map/ppermute | solution.py:32
  179.1 36.8 %collective-permute-start.40 = (bf16[768,512]{1,0:T(8,128)(2,1)S(1)}, bf16[768,512]{1,0:T(8,128)(2,1)S(1)}, u32[]{:S(2)}, u32[]{:S(2)}) collective-permute-start(bf16[768,512]{1,0:T(8,128)(2,1)S(1)} %get-tuple-element.123), channel_id=1, source_target_pairs={{0,64},{64,0},{1,65},{65,1},{2,66},{66,2},{3,67},{67,3},{4,68},{68... | collective-permute-start | bytes 2359304 | tf_op jit(solution)/shard_map/ppermute | solution.py:40
  186.1 23.8 %collective-permute-start.46 = (bf16[480,256]{1,0:T(8,128)(2,1)S(1)}, bf16[480,256]{1,0:T(8,128)(2,1)S(1)}, u32[]{:S(2)}, u32[]{:S(2)}) collective-permute-start(bf16[480,256]{1,0:T(8,128)(2,1)S(1)} %slice.91), channel_id=1, source_target_pairs={{0,16},{16,32},{32,48},{48,0},{1,17},{17,33},{33,49},{49,1},{2,18}... | collective-permute-start | bytes 737288 | tf_op jit(solution)/shard_map/ppermute | solution.py:32
  186.8 23.2 %collective-permute-start.47 = (bf16[480,256]{1,0:T(8,128)(2,1)S(1)}, bf16[480,256]{1,0:T(8,128)(2,1)S(1)}, u32[]{:S(2)}, u32[]{:S(2)}) collective-permute-start(bf16[480,256]{1,0:T(8,128)(2,1)S(1)} %slice.92), channel_id=1, source_target_pairs={{0,16},{16,32},{32,48},{48,0},{1,17},{17,33},{33,49},{49,1},{2,18}... | collective-permute-start | bytes 737288 | tf_op jit(solution)/shard_map/ppermute | solution.py:32
  207.3 24.7 %collective-permute-start.45 = (bf16[768,512]{1,0:T(8,128)(2,1)S(1)}, bf16[768,512]{1,0:T(8,128)(2,1)S(1)}, u32[]{:S(2)}, u32[]{:S(2)}) collective-permute-start(bf16[768,512]{1,0:T(8,128)(2,1)S(1)} %get-tuple-element.131), channel_id=1, source_target_pairs={{0,64},{64,0},{1,65},{65,1},{2,66},{66,2},{3,67},{67,3},{4,68},{68... | collective-permute-start | bytes 2359304 | tf_op jit(solution)/shard_map/ppermute | solution.py:40
  214.9 16.9 %collective-permute-start.50 = (bf16[480,512]{1,0:T(8,128)(2,1)S(1)}, bf16[480,512]{1,0:T(8,128)(2,1)S(1)}, u32[]{:S(2)}, u32[]{:S(2)}) collective-permute-start(bf16[480,512]{1,0:T(8,128)(2,1)S(1)} %get-tuple-element.139), channel_id=1, source_target_pairs={{0,64},{64,0},{1,65},{65,1},{2,66},{66,2},{3,67},{67,3},{4,68},{68... | collective-permute-start | bytes 1474568 | tf_op jit(solution)/shard_map/ppermute | solution.py:40
  (52 other events, 515.5 us)
Sparse Core Ops, SparseCore 0:
  132.0 47.2 reduce-scatter.1
where the time goes:
time: 243 us; the launch traced here: 241 us
  waiting for transfers between devices  74.8 us (31%)
  Pallas kernels  64.4 us (27%)
  starting transfers between devices  62.7 us (26%)
  local copies, waits for them, and re-layouts  17.4 us (7%)
  between operations  14.5 us (6%)
  other arithmetic  7.7 us (3%)
    ppermute x21, waiting for transfers between devices, send_x(): return lax.ppermute(a, 'x', ring(4, step))  45.6 us
    ppermute x21, starting transfers between devices, send_x(): return lax.ppermute(a, 'x', ring(4, step))  29.3 us
    pallas_call x2, Pallas kernels, hidden_call(): pl.pallas_call(functools.partial(hidden_kernel, places), grid=(N_TILES,),...  25.9 us
    pallas_call x4, Pallas kernels, weights_call(): pl.pallas_call(functools.partial(weights_kernel, n, [s for _, s in pieces...  24.4 us
    ppermute x10, starting transfers between devices, send_z(): return lax.ppermute(a, 'z', ring(4, step))  17.3 us
    ppermute x20, waiting for transfers between devices, swap(): return lax.ppermute(a, axis, [(0, 1), (1, 0)])  16.3 us
    ppermute x20, starting transfers between devices, swap(): return lax.ppermute(a, axis, [(0, 1), (1, 0)])  16.1 us
    pallas_call x1, Pallas kernels, in_grads_call(): pl.pallas_call(in_grads_kernel, grid_spec=pltpu.PrefetchScalarGridSpec(nu...  14.1 us
  transfers between devices with their start and end apart: 52, of which 13 were waited for; matrix products, arithmetic and copies ran while one was open for 5% of the time, Pallas kernels for 21%

commit v1 on v0

--- a/solution.py
+++ b/solution.py
@@ -12,15 +12,16 @@
 TILE = 256
 N_TILES = 4
 LAST = 160
-ROWS = 3 * (3 * TILE + LAST)
+UNITS = (TILE, TILE, TILE, LAST)
 BF = jnp.bfloat16
 F32 = jnp.float32
-VMEM_LIMIT = 48 * 1024 * 1024
+MIB = 1024 * 1024
 ANY = pl.BlockSpec(memory_space=pl.ANY)
 COST = 8
 
 
 ORDER = (((0, 0), (0, 1), (0, 3), (1, 0)), ((0, 2), (1, 2), (1, 1), (1, 3)))
+SOURCES = (0, 3, 1, 2)
 SLOT = {step: (b, k) for b in range(2) for k, step in enumerate(ORDER[b])}
 
 
@@ -44,12 +45,14 @@
     return lax.dot_general(a, b, (((ca,), (cb,)), ((), ())), preferred_element_type=F32)
 
 
-def after(a, *others):
-    return lax.optimization_barrier((a, *others))[0]
-
-
-def hidden_kernel(places, *refs):
-    pieces, (wg_ref, wu_ref, wd_ref, dt_ref, dn_ref, tok, sems) = refs[:-7], refs[-7:]
+def hidden_kernel(places, outs, *refs):
+    n = len(outs)
+    pieces, (wg_ref, wu_ref, wd_ref), dt_refs, (dn_ref, tok, sems) = (
+        refs[: -6 - n],
+        refs[-6 - n : -3 - n],
+        refs[-3 - n : -3],
+        refs[-3:],
+    )
     j = pl.program_id(0)
 
     @pl.when(j == 0)
@@ -84,35 +87,34 @@
     dn_ref[0] = d_gate.T
     dn_ref[1] = d_up.T
 
-    @pl.when(j < N_TILES - 1)
-    def _():
-        dt_ref[:TILE] = d_gate
-        dt_ref[TILE : 2 * TILE] = d_up
-        dt_ref[2 * TILE :] = hidden
-
-    @pl.when(j == N_TILES - 1)
-    def _():
-        dt_ref[:LAST] = d_gate[:LAST]
-        dt_ref[LAST : 2 * LAST] = d_up[:LAST]
-        dt_ref[2 * LAST : 3 * LAST] = hidden[:LAST]
-
-
-def hidden_call(pieces, places, wg_rows, wu_rows, w_down):
+    for dt_ref, tiles in zip(dt_refs, outs):
+        for i, tile in enumerate(tiles):
+
+            @pl.when(j == tile)
+            def _():
+                n = UNITS[tile]
+                for part, value in enumerate((d_gate, d_up, hidden)):
+                    row = 3 * TILE * i + n * part
+                    dt_ref[row : row + n] = value[:n]
+
+
+def hidden_call(pieces, places, outs, wg_rows, wu_rows, w_down):
+    rows = [sum(3 * UNITS[t] for t in tiles) for tiles in outs]
     weight = pl.BlockSpec((TILE, D), lambda j: (j, 0))
     return pl.pallas_call(
-        functools.partial(hidden_kernel, places),
+        functools.partial(hidden_kernel, places, outs),
         grid=(N_TILES,),
         in_specs=[ANY] * len(pieces) + [weight] * 3,
         out_specs=[
-            pl.BlockSpec((3 * TILE, 256), lambda j: (j, 0)),
+            *[pl.BlockSpec((r, 256), lambda j: (0, 0)) for r in rows],
             pl.BlockSpec((2, 256, TILE), lambda j: (0, 0, j)),
         ],
         out_shape=[
-            jax.ShapeDtypeStruct((ROWS, 256), BF),
+            *[jax.ShapeDtypeStruct((r, 256), BF) for r in rows],
             jax.ShapeDtypeStruct((2, 256, FF), BF),
         ],
         scratch_shapes=[pltpu.VMEM((2, 256, D), BF), pltpu.SemaphoreType.DMA((16,))],
-        compiler_params=pltpu.CompilerParams(vmem_limit_bytes=VMEM_LIMIT),
+        compiler_params=pltpu.CompilerParams(vmem_limit_bytes=48 * MIB),
         cost_estimate=pl.CostEstimate(
             flops=6 * 256 * D * FF // COST, bytes_accessed=6 * D * FF // COST, transcendentals=0
         ),
@@ -133,14 +135,14 @@
         for c, out_ref in enumerate((own_ref, other_ref)):
             for i, (y_step, z_step) in enumerate(ORDER[b]):
                 row = 256 * b + 128 * c + 32 * i
-                out_ref[y_step ^ yl, lax.rem(z_step + z, 4)] = p[row : row + 32]
+                out_ref[lax.rem(z_step + z, 4), y_step ^ yl] = p[row : row + 32]
 
 
 def in_grads_call(pos, dn0, dn1, wg_rows, wu_rows):
     cols = 512
     whole = pl.BlockSpec((2, 256, FF), lambda j, p: (0, 0, 0))
     weight = pl.BlockSpec((FF, cols), lambda j, p: (0, j))
-    out = pl.BlockSpec((2, 4, 32, cols), lambda j, p: (0, 0, 0, j))
+    out = pl.BlockSpec((4, 2, 32, cols), lambda j, p: (0, 0, 0, j))
     return pl.pallas_call(
         in_grads_kernel,
         grid_spec=pltpu.PrefetchScalarGridSpec(
@@ -150,8 +152,8 @@
             out_specs=[out, out],
             scratch_shapes=[pltpu.VMEM((2, 512, FF), BF)],
         ),
-        out_shape=[jax.ShapeDtypeStruct((2, 4, 32, D), BF)] * 2,
-        compiler_params=pltpu.CompilerParams(vmem_limit_bytes=VMEM_LIMIT),
+        out_shape=[jax.ShapeDtypeStruct((4, 2, 32, D), BF)] * 2,
+        compiler_params=pltpu.CompilerParams(vmem_limit_bytes=48 * MIB),
         cost_estimate=pl.CostEstimate(
             flops=4 * 512 * D * FF // COST, bytes_accessed=4 * D * FF // COST, transcendentals=0
         ),
@@ -159,9 +161,16 @@
     )(pos, dn0, dn1, wg_rows, wu_rows)
 
 
-def weights_kernel(n, starts, *refs):
-    pieces, col_pieces = refs[:8], refs[8:18]
-    send_ref, keep_ref, stack, x, sems = refs[18:]
+def weights_kernel(n, places, pos_ref, *refs):
+    pieces, col_pieces = refs[:5], refs[5:15]
+    send_ref, keep_ref, stack, x, sems = refs[15:]
+    start, stride, second = places
+    sources = []
+    for step in SOURCES:
+        first = lax.rem(pos_ref[2] + step, 4) * stride + start
+        sources.append(pieces[0].at[pl.ds(pl.multiple_of(first, 32), 3 * n), :])
+    sources += [ref.at[pl.ds(second, 3 * n), :] for ref in pieces[1:4]]
+    sources.append(pieces[4])
     halves = ([], [])
     count = [0]
 
@@ -174,11 +183,7 @@
     for b in range(2):
         for s in range(4):
             i = 4 * b + s
-            put(
-                halves[0],
-                pieces[i].at[pl.ds(starts[i], 3 * n), :],
-                stack.at[b, :, pl.ds(256 * s, 256)],
-            )
+            put(halves[0], sources[i], stack.at[b, :, pl.ds(256 * s, 256)])
     for h in range(2):
         cols = pl.ds(512 * h, 512)
         for c in range(2):
@@ -206,10 +211,10 @@
         out_ref[2 * n :] = total(slice(2 * n, 3 * n), 1)
 
 
-def weights_call(n, pieces, col_pieces):
+def weights_call(n, pos, places, pieces, col_pieces):
     return pl.pallas_call(
-        functools.partial(weights_kernel, n, [s for _, s in pieces]),
-        in_specs=[ANY] * 18,
+        functools.partial(weights_kernel, n, places),
+        in_specs=[pl.BlockSpec(memory_space=pltpu.SMEM)] + [ANY] * 15,
         out_specs=[pl.BlockSpec(memory_space=pltpu.VMEM)] * 2,
         out_shape=[jax.ShapeDtypeStruct((3 * n, 512), BF)] * 2,
         scratch_shapes=[
@@ -217,12 +222,12 @@
             pltpu.VMEM((2, 2, 4, 2, 4, 32, 1024), BF),
             pltpu.SemaphoreType.DMA((48,)),
         ],
-        compiler_params=pltpu.CompilerParams(vmem_limit_bytes=VMEM_LIMIT),
+        compiler_params=pltpu.CompilerParams(vmem_limit_bytes=48 * MIB),
         cost_estimate=pl.CostEstimate(
             flops=6 * n * 2048 * 1024 // COST, bytes_accessed=(12 << 20) // COST, transcendentals=0
         ),
         name="weight_grads",
-    )(*[a for a, _ in pieces], *col_pieces)
+    )(pos, *pieces, *col_pieces)
 
 
 def gate(*arrays):
@@ -235,7 +240,7 @@
 
 def on_device(inputs, out_grads, w_gate, w_up, w_down):
     xi, yh, yl, zi = (lax.axis_index(a) for a in ("x", "yh", "yl", "z"))
-    pos = jnp.stack([yl, zi]).astype(jnp.int32)
+    pos = jnp.stack([yl, zi, xi]).astype(jnp.int32)
     wg_rows, wu_rows = w_gate.T, w_up.T
     mine = jnp.stack([inputs, out_grads])
 
@@ -255,19 +260,10 @@
     batch0 = [mine, left, right, partner]
     batch0 += core_swaps(batch0)
     both = ((None, 0),), ((None, 1),), ((None, 2),), ((None, 3),)
-    dt0, dn0 = hidden_call(batch0, both, wg_rows, wu_rows, w_down)
-    dt0, dn0, p_right, p_left, shares, other_shares = gate(dt0, dn0, p_right, p_left, shares, other_shares)
-
-    lanes = {1: [], -1: []}
-
-    def in_turn(a, step):
-        lane = lanes[step]
-        if len(lane) >= 2:
-            a = after(a, lane[-2])
-        lane.append(send_x(a, step))
-        return lane[-1]
-
-    right0, left0 = in_turn(dt0, 1), in_turn(dt0, -1)
+    own0, dn0 = hidden_call(batch0, both, ((0, 1, 2, 3),), wg_rows, wu_rows, w_down)
+    own0, dn0, p_right, p_left, shares, other_shares = gate(own0, dn0, p_right, p_left, shares, other_shares)
+    gathered0 = lax.all_gather(own0, "x", axis=0, tiled=True)
+
     far_in = send_z(jnp.stack([right[0], p_right[0]]), 1)
     far_grad = send_z(jnp.stack([left[1], p_left[1]]), -1)
     batch1 = [far_in, far_grad, p_left, p_right]
@@ -276,38 +272,54 @@
     shares, *batch1 = gate(shares, *batch1)
 
     places = ((0, 0), (0, 1)), ((1, 0), (1, 1)), ((None, 2),), ((None, 3),)
-    dt1, dn1 = hidden_call(batch1, places, wg_rows, wu_rows, w_down)
+    *own1, dn1 = hidden_call(batch1, places, ((0, 1), (2, 3)), wg_rows, wu_rows, w_down)
     c_right, c_left = send_z(shares, 1), send_z(shares, -1)
-    dt1, dn1, c_right, c_left, right0, left0 = gate(dt1, dn1, c_right, c_left, right0, left0)
-
+    right1, left1 = [send_x(own1[0], 1)], [send_x(own1[0], -1)]
+    cut = 3 * TILE
+    c_far_in, c_far_grad = send_z(c_right[:, 0], 1), send_z(c_left[:, 1], -1)
+    shares_other = swap(shares, "core")
     term_own, term_other = in_grads_call(pos, dn0, dn1, wg_rows, wu_rows)
-    col_pieces = [shares, c_left, send_z(c_right[:, 0], 1), send_z(c_left[:, 1], -1), c_right]
-    col_pieces += core_swaps(col_pieces)
-
-    kept, sent = [], []
-    for j in range(N_TILES):
-        n = TILE if j < N_TILES - 1 else LAST
-        start = 3 * TILE * j
-        rows = slice(start, start + 3 * n)
-        right0_rows, dt1_rows = right0[rows], dt1[rows]
-        if j == 1:
-            term_own, term_other, right0_rows, dt1_rows = gate(term_own, term_other, right0_rows, dt1_rows)
-        if j >= 2:
-            send, keep, right0_rows, dt1_rows = gate(sent[j - 2], kept[j - 2], right0_rows, dt1_rows)
-            sent[j - 2], kept[j - 2] = send, keep
-        far0, left1 = in_turn(right0_rows, 1), in_turn(dt1_rows, -1)
-        right1, far1 = in_turn(dt1_rows, 1), in_turn(left1, -1)
-        pieces = [
-            (dt0, start), (right0, start), (left0, start), (far0, 0),
-            (dt1, start), (right1, 0), (left1, 0), (far1, 0),
-        ]
-        send, keep = weights_call(n, pieces, col_pieces)
+    term_own, term_other, c_far_in, c_far_grad, right1[0], left1[0], own1[1], shares_other, c_left, c_right, gathered0 = gate(
+        term_own, term_other, c_far_in, c_far_grad, right1[0], left1[0], own1[1], shares_other, c_left, c_right, gathered0
+    )
+
+    far1 = [send_x(right1[0][:cut], 1), send_x(left1[0][cut:], -1)]
+    c_here = [c_left, c_far_in, c_far_grad, c_right]
+    c_other = core_swaps(c_here)
+    term_other = swap(term_other, "core")
+    *far1, own1[1], term_other = gate(*far1, own1[1], term_other, *c_other)[:4]
+    col_pieces = [shares, *c_here, shares_other, *c_other]
+    kept, sent, got = [], [], []
+
+    def weights(j):
+        side, start = j // 2, cut * (j % 2)
+        pieces = [gathered0, own1[side], right1[side], left1[side], far1[j]]
+        send, keep = weights_call(UNITS[j], pos, (cut * j, own0.shape[0], start), pieces, col_pieces)
         kept.append(keep)
         sent.append(send)
 
-    sent = [swap(a, "yh") for a in sent]
-    pair = (term_own.astype(F32) + swap(term_other, "core").astype(F32)).astype(BF)
-    in_grads = lax.psum_scatter(pair.reshape(256, D), ("yl", "z"), scatter_dimension=0, tiled=True)
+    right1.append(send_x(own1[1], 1))
+    left1.append(send_x(own1[1], -1))
+    weights(0)
+    sent[0], own1[0], term_other = gate(sent[0], own1[0], term_other)
+    pair = (term_own.astype(F32) + term_other.astype(F32)).astype(BF)
+    scattered = lax.psum_scatter(pair.reshape(256, D), "z", scatter_dimension=0, tiled=True)
+    got.append(swap(sent[0], "yh"))
+    weights(1)
+    right1[1], left1[1], sent[1] = gate(right1[1], left1[1], sent[1])
+    got.append(swap(sent[1], "yh"))
+    far1 += [send_x(right1[1][:cut], 1), send_x(left1[1][cut:], -1)]
+    scattered = scattered.reshape(2, 32, D)
+    mine_part = lax.dynamic_index_in_dim(scattered, yl, axis=0, keepdims=False)
+    other_part = lax.dynamic_index_in_dim(scattered, 1 - yl, axis=0, keepdims=False)
+    in_grads = (mine_part.astype(F32) + swap(other_part, "yl").astype(F32)).astype(BF)
+    far1[2], far1[3], got[0], own1[1] = gate(far1[2], far1[3], got[0], own1[1])
+    weights(2)
+    got.append(swap(sent[2], "yh"))
+    got[1], sent[2], own1[1] = gate(got[1], sent[2], own1[1])
+    weights(3)
+    got.append(swap(sent[3], "yh"))
+    sent = got
 
     gate_parts, up_parts, down_parts = [], [], []
     for j in range(N_TILES):

time: 243 us -> 240 us (0.988)
  starting transfers between devices: 62.7 us -> 48.4 us
  local copies, waits for them, and re-layouts: 17.4 us -> 22.9 us
  other arithmetic: 7.7 us -> 11.8 us
  Pallas kernels: 64.4 us -> 67.8 us
    ppermute x21 -> x11, waiting for transfers between devices: 45.6 us -> 28.4 us  [send_x(): return lax.ppermute(a, 'x', ring(4, step))]
    ppermute x21 -> x11, starting transfers between devices: 29.3 us -> 18.5 us  [send_x(): return lax.ppermute(a, 'x', ring(4, step))]
    unnamed x48 -> x80, local copies, waits for them, and re-layouts: 8.74 us -> 17.2 us
    ppermute x10, waiting for transfers between devices: 12.9 us -> 20 us  [send_z(): return lax.ppermute(a, 'z', ring(4, step))]
    ppermute x20 -> x21, waiting for transfers between devices: 16.3 us -> 23 us  [swap(): return lax.ppermute(a, axis, [(0, 1), (1, 0)])]
    pallas_call x6, Pallas kernels: 50.3 us -> 53.6 us  [the longest x4 27.3 us: weights_call(): pl.pallas_call(functools.partial(weights_kernel, n, places), in_specs=[pl...]
    slice x4, local copies, waits for them, and re-layouts: 5.63 us -> 2.59 us  [the longest x2 1.55 us: on_device(): far1 += [send_x(right1[1][:cut], 1), send_x(left1[1][cut:], -1)]]
    ppermute x10, starting transfers between devices: 17.3 us -> 14.6 us  [send_z(): return lax.ppermute(a, 'z', ring(4, step))]
  transfers between devices with their start and end apart: 52 -> 44, of which waited for: 13 -> 19; matrix products, arithmetic and copies ran while one was open for 5% -> 5% of each run, Pallas kernels for 21% -> 25%
where the time goes in v1:
time: 240 us; the launch traced here: 239 us
  waiting for transfers between devices  73.6 us (31%)
  Pallas kernels  67.8 us (28%)
  starting transfers between devices  48.4 us (20%)
  local copies, waits for them, and re-layouts  22.9 us (10%)
  between operations  14.5 us (6%)
  other arithmetic  11.8 us (5%)
    ppermute x11, waiting for transfers between devices, send_x(): return lax.ppermute(a, 'x', ring(4, step))  28.4 us
    pallas_call x4, Pallas kernels, weights_call(): pl.pallas_call(functools.partial(weights_kernel, n, places), in_specs=[pl...  27.3 us
    pallas_call x2, Pallas kernels, hidden_call(): pl.pallas_call(functools.partial(hidden_kernel, places, outs), grid=(N_TI...  26.3 us
    ppermute x21, waiting for transfers between devices, swap(): return lax.ppermute(a, axis, [(0, 1), (1, 0)])  23 us
    ppermute x10, waiting for transfers between devices, send_z(): return lax.ppermute(a, 'z', ring(4, step))  20 us
    ppermute x11, starting transfers between devices, send_x(): return lax.ppermute(a, 'x', ring(4, step))  18.5 us
    unnamed x80, local copies, waits for them, and re-layouts  17.2 us
    ppermute x21, starting transfers between devices, swap(): return lax.ppermute(a, axis, [(0, 1), (1, 0)])  15.2 us
  transfers between devices with their start and end apart: 44, of which 19 were waited for; matrix products, arithmetic and copies ran while one was open for 5% of the time, Pallas kernels for 25%

profile of v1, /device:TPU:0, one launch (start us, length us, event | category | flops | bytes accessed | tf_op | source)
XLA Modules:
  0.0 239.0 jit_solution(13679720386781876426)
XLA Ops:
  18.6 2.8 %collective-permute-done.3 = bf16[2,32,1024]{2,1,0:T(8,128)(2,1)S(1)} collective-permute-done((bf16[2,32,1024]{2,1,0:T(8,128)(2,1)S(1)}, bf16[2,32,1024]{2,1,0:T(8,128)(2,1)S(1)}, u32[]{:S(2)}, u32[]{:S(2)}) %collective-permute-start.3) | collective-permute-done | bytes 131104 | tf_op jit(solution)/shard_map/ppermute | solution.py:33
  23.4 4.5 %collective-permute-done.5 = bf16[2,32,1024]{2,1,0:T(8,128)(2,1)S(1)} collective-permute-done((bf16[2,32,1024]{2,1,0:T(8,128)(2,1)S(1)}, bf16[2,32,1024]{2,1,0:T(8,128)(2,1)S(1)}, u32[]{:S(2)}, u32[]{:S(2)}) %collective-permute-start.5) | collective-permute-done | bytes 131104 | tf_op jit(solution)/shard_map/ppermute | solution.py:33
  29.9 2.5 %collective-permute-start.11 = (bf16[2,32,4096]{2,1,0:T(8,128)(2,1)S(1)}, bf16[2,32,4096]{2,1,0:T(8,128)(2,1)S(1)}, u32[]{:S(2)}, u32[]{:S(2)}) collective-permute-start(bf16[2,32,4096]{2,1,0:T(8,128)(2,1)S(1)} %collective-permute-done.2.refs_3_), channel_id=1, source_target_pairs={{0,6},{2,0},{4,2},{6,4},{1,7},{3,1},{5,3},{7,5},{8,14},{10,8},{12,... | collective-permute-start | bytes 1572872 | tf_op jit(solution)/shard_map/ppermute | solution.py:37
  32.4 13.3 %hidden_grads.2 = (bf16[2784,256]{1,0:T(8,128)(2,1)}, bf16[2,256,924]{2,1,0:T(8,128)(2,1)S(1)}) custom-call(bf16[2,32,4096]{2,1,0:T(8,128)(2,1)S(1)} %pad_maximum_fusion.refs_0_, bf16[2,32,4096]{2,1,0:T(8,128)(2,1)S(1)} %collective-permute-done.1.refs_1_, bf16[2,32,4096]{2,1,0:T(8,128)(2,1)S(1)} %collective-permute-done.refs_2_, ...), custom_call_target="tpu_custom_call" | custom-call | flops 726663168 | bytes 2838528 | tf_op jit(solution)/shard_map/hidden_grads/pallas_call | solution.py:104
  50.5 11.1 %collective-permute-done.14.refs_1_ = bf16[2,32,4096]{2,1,0:T(8,128)(2,1)S(1)} collective-permute-done((bf16[2,32,4096]{2,1,0:T(8,128)(2,1)S(1)}, bf16[2,32,4096]{2,1,0:T(8,128)(2,1)S(1)}, u32[]{:S(2)}, u32[]{:S(2)}) %collective-permute-start.14) | collective-permute-done | bytes 524320 | tf_op jit(solution)/shard_map/ppermute | solution.py:37
  61.6 2.5 %collective-permute-done.13.refs_0_ = bf16[2,32,4096]{2,1,0:T(8,128)(2,1)S(1)} collective-permute-done((bf16[2,32,4096]{2,1,0:T(8,128)(2,1)S(1)}, bf16[2,32,4096]{2,1,0:T(8,128)(2,1)S(1)}, u32[]{:S(2)}, u32[]{:S(2)}) %collective-permute-start.13) | collective-permute-done | bytes 524320 | tf_op jit(solution)/shard_map/ppermute | solution.py:37
  66.0 3.2 %collective-permute-start.21 = (bf16[2,2,4,32,1024]{4,3,2,1,0:T(8,128)(2,1)}, bf16[2,2,4,32,1024]{4,3,2,1,0:T(8,128)(2,1)S(1)}, u32[]{:S(2)}, u32[]{:S(2)}) collective-permute-start(bf16[2,2,4,32,1024]{4,3,2,1,0:T(8,128)(2,1)} %pad_maximum_fusion.1.refs_5_), channel_id=1, source_target_pairs={{0,6},{2,0},{4,2},{6,4},{1,7},{3,1},{5,3},{7,5},{8,14},{10,8},{12,... | collective-permute-start | bytes 3145736 | tf_op jit(solution)/shard_map/ppermute | solution.py:37
  69.3 13.0 %hidden_grads.3 = (bf16[1536,256]{1,0:T(8,128)(2,1)S(1)}, bf16[1248,256]{1,0:T(8,128)(2,1)S(1)}, bf16[2,256,924]{2,1,0:T(8,128)(2,1)}) custom-call(bf16[2,32,4096]{2,1,0:T(8,128)(2,1)S(1)} %collective-permute-done.13.refs_0_, bf16[2,32,4096]{2,1,0:T(8,128)(2,1)S(1)} %collective-permute-done.14.refs_1_, bf16[2,32,4096]{2,1,0:T(8,128)(2,1)S(1)} %copy-done.11, ...), custom_call_target="tpu_custom_call" | custom-call | flops 726663168 | bytes 2838528 | tf_op jit(solution)/shard_map/hidden_grads/pallas_call | solution.py:104
  83.4 2.9 %collective-permute-start.24 = (bf16[1536,256]{1,0:T(8,128)(2,1)S(1)}, bf16[1536,256]{1,0:T(8,128)(2,1)}, u32[]{:S(2)}, u32[]{:S(2)}) collective-permute-start(bf16[1536,256]{1,0:T(8,128)(2,1)S(1)} %get-tuple-element.114.refs_1_), channel_id=1, source_target_pairs={{0,48},{16,0},{32,16},{48,32},{1,49},{17,1},{33,17},{49,33},{2,50}... | collective-permute-start | bytes 2359304 | tf_op jit(solution)/shard_map/ppermute | solution.py:33
  86.3 6.3 %collective-permute-done.19.refs_9_ = bf16[2,2,4,32,1024]{4,3,2,1,0:T(8,128)(2,1)S(1)} collective-permute-done((bf16[2,2,4,32,1024]{4,3,2,1,0:T(8,128)(2,1)}, bf16[2,2,4,32,1024]{4,3,2,1,0:T(8,128)(2,1)S(1)}, u32[]{:S(2)}, u32[]{:S(2)}) %collective-permute-start.19) | collective-permute-done | bytes 1048608 | tf_op jit(solution)/shard_map/ppermute | solution.py:37
  94.8 2.4 collective-permute-start.22
  99.7 14.2 %in_grads_terms.1 = (bf16[4,2,32,4096]{3,2,1,0:T(8,128)(2,1)S(1)}, bf16[4,2,32,4096]{3,2,1,0:T(8,128)(2,1)}) custom-call(s32[3]{0:T(128)S(1)} %pad_add_fusion.pos_ref, bf16[2,256,924]{2,1,0:T(8,128)(2,1)S(1)} %copy-done.13, bf16[2,256,924]{2,1,0:T(8,128)(2,1)S(1)} %copy-done.14, bf16[924,4096]{1,0:T(8,128)(2,1)} %bitcast.36, bf16[924,4096]{1,0:T(8,128)(2,1)} %bitcast.39), custom_call_target="tpu_custom_call" | custom-call | flops 968884224 | bytes 1892352 | tf_op jit(solution)/shard_map/in_grads_terms/pallas_call | solution.py:146
  115.2 6.2 %collective-permute-done.23.refs_2_ = bf16[1536,256]{1,0:T(8,128)(2,1)S(1)} collective-permute-done((bf16[1536,256]{1,0:T(8,128)(2,1)S(1)}, bf16[1536,256]{1,0:T(8,128)(2,1)S(1)}, u32[]{:S(2)}, u32[]{:S(2)}) %collective-permute-start.23) | collective-permute-done | bytes 786464 | tf_op jit(solution)/shard_map/ppermute | solution.py:33
  128.5 8.4 %collective-permute-done.26.refs_4_ = bf16[768,256]{1,0:T(8,128)(2,1)S(1)} collective-permute-done((bf16[768,256]{1,0:T(8,128)(2,1)S(1)}, bf16[768,256]{1,0:T(8,128)(2,1)S(1)}, u32[]{:S(2)}, u32[]{:S(2)}) %collective-permute-start.26) | collective-permute-done | bytes 393248 | tf_op jit(solution)/shard_map/ppermute | solution.py:33
  141.6 7.1 %weight_grads.4 = (bf16[768,512]{1,0:T(8,128)(2,1)S(1)}, bf16[768,512]{1,0:T(8,128)(2,1)S(1)}) custom-call(s32[3]{0:T(128)S(1)} %pad_add_fusion.pos_ref, bf16[11136,256]{1,0:T(8,128)(2,1)} %all-gather.2.cloned.1.call-done.refs_0_, bf16[1536,256]{1,0:T(8,128)(2,1)S(1)} %copy-done.3, bf16[1536,256]{1,0:T(8,128)(2,1)S(1)} %collective-permute-done.23.refs_2_, ...), custom_call_target="tpu_custom_call" | custom-call | flops 402653184 | bytes 1572864 | tf_op jit(solution)/shard_map/weight_grads/pallas_call | solution.py:215
  154.4 3.0 %collective-permute-start.38 = (bf16[768,512]{1,0:T(8,128)(2,1)}, bf16[768,512]{1,0:T(8,128)(2,1)}, u32[]{:S(2)}, u32[]{:S(2)}) collective-permute-start(bf16[768,512]{1,0:T(8,128)(2,1)} %copy-done.25), channel_id=1, source_target_pairs={{0,64},{64,0},{1,65},{65,1},{2,66},{66,2},{3,67},{67,3},{4,68},{68... | collective-permute-start | bytes 2359304 | tf_op jit(solution)/shard_map/ppermute | solution.py:41
  159.6 7.5 %weight_grads.5 = (bf16[768,512]{1,0:T(8,128)(2,1)}, bf16[768,512]{1,0:T(8,128)(2,1)S(1)}) custom-call(s32[3]{0:T(128)S(1)} %pad_add_fusion.pos_ref, bf16[11136,256]{1,0:T(8,128)(2,1)} %all-gather.2.cloned.1.call-done.refs_0_, bf16[1536,256]{1,0:T(8,128)(2,1)S(1)} %copy-done.4, bf16[1536,256]{1,0:T(8,128)(2,1)S(1)} %collective-permute-done.23.refs_2_, ...), custom_call_target="tpu_custom_call" | custom-call | flops 402653184 | bytes 1572864 | tf_op jit(solution)/shard_map/weight_grads/pallas_call | solution.py:215
  174.0 3.0 %collective-permute-start.39 = (bf16[768,512]{1,0:T(8,128)(2,1)}, bf16[768,512]{1,0:T(8,128)(2,1)}, u32[]{:S(2)}, u32[]{:S(2)}) collective-permute-start(bf16[768,512]{1,0:T(8,128)(2,1)} %get-tuple-element.122), channel_id=1, source_target_pairs={{0,64},{64,0},{1,65},{65,1},{2,66},{66,2},{3,67},{67,3},{4,68},{68... | collective-permute-start | bytes 2359304 | tf_op jit(solution)/shard_map/ppermute | solution.py:41
  186.1 7.0 %weight_grads.6 = (bf16[768,512]{1,0:T(8,128)(2,1)S(1)}, bf16[768,512]{1,0:T(8,128)(2,1)S(1)}) custom-call(s32[3]{0:T(128)S(1)} %pad_add_fusion.pos_ref, bf16[11136,256]{1,0:T(8,128)(2,1)} %all-gather.2.cloned.1.call-done.refs_0_, bf16[1248,256]{1,0:T(8,128)(2,1)S(1)} %copy-done.6, bf16[1248,256]{1,0:T(8,128)(2,1)S(1)} %collective-permute-done.34.refs_2_, ...), custom_call_target="tpu_custom_call" | custom-call | flops 402653184 | bytes 1572864 | tf_op jit(solution)/shard_map/weight_grads/pallas_call | solution.py:215
  193.1 3.1 %collective-permute-start.40 = (bf16[768,512]{1,0:T(8,128)(2,1)S(1)}, bf16[768,512]{1,0:T(8,128)(2,1)S(1)}, u32[]{:S(2)}, u32[]{:S(2)}) collective-permute-start(bf16[768,512]{1,0:T(8,128)(2,1)S(1)} %get-tuple-element.125), channel_id=1, source_target_pairs={{0,64},{64,0},{1,65},{65,1},{2,66},{66,2},{3,67},{67,3},{4,68},{68... | collective-permute-start | bytes 2359304 | tf_op jit(solution)/shard_map/ppermute | solution.py:41
  198.6 5.7 %weight_grads.7 = (bf16[480,512]{1,0:T(8,128)(2,1)S(1)}, bf16[480,512]{1,0:T(8,128)(2,1)S(1)}) custom-call(s32[3]{0:T(128)S(1)} %pad_add_fusion.pos_ref, bf16[11136,256]{1,0:T(8,128)(2,1)} %all-gather.2.cloned.1.call-done.refs_0_, bf16[1248,256]{1,0:T(8,128)(2,1)S(1)} %copy-done.7, bf16[1248,256]{1,0:T(8,128)(2,1)S(1)} %collective-permute-done.34.refs_2_, ...), custom_call_target="tpu_custom_call" | custom-call | flops 251658240 | bytes 1572864 | tf_op jit(solution)/shard_map/weight_grads/pallas_call | solution.py:215
  206.3 8.9 %collective-permute-done.40 = bf16[768,512]{1,0:T(8,128)(2,1)S(1)} collective-permute-done((bf16[768,512]{1,0:T(8,128)(2,1)S(1)}, bf16[768,512]{1,0:T(8,128)(2,1)S(1)}, u32[]{:S(2)}, u32[]{:S(2)}) %collective-permute-start.40) | collective-permute-done | bytes 786464 | tf_op jit(solution)/shard_map/ppermute | solution.py:41
  215.5 8.2 %collective-permute-done.41 = bf16[480,512]{1,0:T(8,128)(2,1)S(1)} collective-permute-done((bf16[480,512]{1,0:T(8,128)(2,1)S(1)}, bf16[480,512]{1,0:T(8,128)(2,1)S(1)}, u32[]{:S(2)}, u32[]{:S(2)}) %collective-permute-start.41) | collective-permute-done | bytes 491552 | tf_op jit(solution)/shard_map/ppermute | solution.py:41
  228.9 2.5 %collective-permute-done.33 = bf16[32,4096]{1,0:T(8,128)(2,1)S(1)} collective-permute-done((bf16[32,4096]{1,0:T(8,128)(2,1)S(1)}, bf16[32,4096]{1,0:T(8,128)(2,1)S(1)}, u32[]{:S(2)}, u32[]{:S(2)}) %collective-permute-start.33) | collective-permute-done | bytes 262176 | tf_op jit(solution)/shard_map/ppermute | solution.py:41
  (188 shorter events, 75.2 us)
Async XLA Ops:
  7.2 116.3 %all-gather.2.cloned.1.call-start = ((), (), s32[]{:S(2)}) async-start(), calls=%async_computation.1 | async-start | bytes 7127040 | tf_op jit(solution)/shard_map/all_gather | solution.py:265
  8.4 19.6 %collective-permute-start = (bf16[2,32,4096]{2,1,0:T(8,128)(2,1)S(1)}, bf16[2,32,4096]{2,1,0:T(8,128)(2,1)S(1)}, u32[]{:S(2)}, u32[]{:S(2)}) collective-permute-start(bf16[2,32,4096]{2,1,0:T(8,128)(2,1)S(1)} %pad_maximum_fusion.refs_0_), channel_id=1, source_target_pairs={{0,2},{2,4},{4,6},{6,0},{1,3},{3,5},{5,7},{7,1},{8,10},{10,12},{12... | collective-permute-start | bytes 1572872 | tf_op jit(solution)/shard_map/ppermute | solution.py:37
  10.4 17.5 %collective-permute-start.1 = (bf16[2,32,4096]{2,1,0:T(8,128)(2,1)S(1)}, bf16[2,32,4096]{2,1,0:T(8,128)(2,1)S(1)}, u32[]{:S(2)}, u32[]{:S(2)}) collective-permute-start(bf16[2,32,4096]{2,1,0:T(8,128)(2,1)S(1)} %pad_maximum_fusion.refs_0_), channel_id=1, source_target_pairs={{0,6},{2,0},{4,2},{6,4},{1,7},{3,1},{5,3},{7,5},{8,14},{10,8},{12,... | collective-permute-start | bytes 1572872 | tf_op jit(solution)/shard_map/ppermute | solution.py:37
  12.6 15.3 %collective-permute-start.2 = (bf16[2,32,4096]{2,1,0:T(8,128)(2,1)S(1)}, bf16[2,32,4096]{2,1,0:T(8,128)(2,1)S(1)}, u32[]{:S(2)}, u32[]{:S(2)}) collective-permute-start(bf16[2,32,4096]{2,1,0:T(8,128)(2,1)S(1)} %pad_maximum_fusion.refs_0_), channel_id=1, source_target_pairs={{0,8},{8,0},{1,9},{9,1},{2,10},{10,2},{3,11},{11,3},{4,12},{12,4},... | collective-permute-start | bytes 1572872 | tf_op jit(solution)/shard_map/ppermute | solution.py:41
  28.5 18.2 %collective-permute-start.10 = (bf16[2,32,4096]{2,1,0:T(8,128)(2,1)S(1)}, bf16[2,32,4096]{2,1,0:T(8,128)(2,1)S(1)}, u32[]{:S(2)}, u32[]{:S(2)}) collective-permute-start(bf16[2,32,4096]{2,1,0:T(8,128)(2,1)S(1)} %collective-permute-done.2.refs_3_), channel_id=1, source_target_pairs={{0,2},{2,4},{4,6},{6,0},{1,3},{3,5},{5,7},{7,1},{8,10},{10,12},{12... | collective-permute-start | bytes 1572872 | tf_op jit(solution)/shard_map/ppermute | solution.py:37
  28.7 18.0 %collective-permute-start.12 = (bf16[2,4,32,1024]{3,2,1,0:T(8,128)(2,1)S(1)}, bf16[2,4,32,1024]{3,2,1,0:T(8,128)(2,1)S(1)}, u32[]{:S(2)}, u32[]{:S(2)}) collective-permute-start(bf16[2,4,32,1024]{3,2,1,0:T(8,128)(2,1)S(1)} %pad_maximum_fusion.3), channel_id=1, source_target_pairs={{0,8},{8,0},{1,9},{9,1},{2,10},{10,2},{3,11},{11,3},{4,12},{12,4},... | collective-permute-start | bytes 1572872 | tf_op jit(solution)/shard_map/ppermute | solution.py:41
  29.9 16.8 %collective-permute-start.11 = (bf16[2,32,4096]{2,1,0:T(8,128)(2,1)S(1)}, bf16[2,32,4096]{2,1,0:T(8,128)(2,1)S(1)}, u32[]{:S(2)}, u32[]{:S(2)}) collective-permute-start(bf16[2,32,4096]{2,1,0:T(8,128)(2,1)S(1)} %collective-permute-done.2.refs_3_), channel_id=1, source_target_pairs={{0,6},{2,0},{4,2},{6,4},{1,7},{3,1},{5,3},{7,5},{8,14},{10,8},{12,... | collective-permute-start | bytes 1572872 | tf_op jit(solution)/shard_map/ppermute | solution.py:37
  47.5 176.4 %reduce-scatter.2.cloned.1.call-start = ((), (), s32[]{:S(2)}) async-start(), calls=%async_computation.2 | async-start | bytes 2621440 | tf_op jit(solution)/shard_map/reduce_scatter | solution.py:306
  66.0 26.6 %collective-permute-start.19 = (bf16[2,2,4,32,1024]{4,3,2,1,0:T(8,128)(2,1)}, bf16[2,2,4,32,1024]{4,3,2,1,0:T(8,128)(2,1)S(1)}, u32[]{:S(2)}, u32[]{:S(2)}) collective-permute-start(bf16[2,2,4,32,1024]{4,3,2,1,0:T(8,128)(2,1)} %pad_maximum_fusion.1.refs_5_), channel_id=1, source_target_pairs={{0,2},{2,4},{4,6},{6,0},{1,3},{3,5},{5,7},{7,1},{8,10},{10,12},{12... | collective-permute-start | bytes 3145736 | tf_op jit(solution)/shard_map/ppermute | solution.py:37
  66.0 26.8 %collective-permute-start.21 = (bf16[2,2,4,32,1024]{4,3,2,1,0:T(8,128)(2,1)}, bf16[2,2,4,32,1024]{4,3,2,1,0:T(8,128)(2,1)S(1)}, u32[]{:S(2)}, u32[]{:S(2)}) collective-permute-start(bf16[2,2,4,32,1024]{4,3,2,1,0:T(8,128)(2,1)} %pad_maximum_fusion.1.refs_5_), channel_id=1, source_target_pairs={{0,6},{2,0},{4,2},{6,4},{1,7},{3,1},{5,3},{7,5},{8,14},{10,8},{12,... | collective-permute-start | bytes 3145736 | tf_op jit(solution)/shard_map/ppermute | solution.py:37
  69.2 52.1 %collective-permute-start.25 = (bf16[2,2,4,32,1024]{4,3,2,1,0:T(8,128)(2,1)}, bf16[2,2,4,32,1024]{4,3,2,1,0:T(8,128)(2,1)}, u32[]{:S(2)}, u32[]{:S(2)}) collective-permute-start(bf16[2,2,4,32,1024]{4,3,2,1,0:T(8,128)(2,1)} %pad_maximum_fusion.1.refs_5_), channel_id=1, source_target_pairs={{0,1},{1,0},{2,3},{3,2},{4,5},{5,4},{6,7},{7,6},{8,9},{9,8},{10,11... | collective-permute-start | bytes 3145736 | tf_op jit(solution)/shard_map/ppermute | solution.py:41
  83.1 38.3 %collective-permute-start.23 = (bf16[1536,256]{1,0:T(8,128)(2,1)S(1)}, bf16[1536,256]{1,0:T(8,128)(2,1)S(1)}, u32[]{:S(2)}, u32[]{:S(2)}) collective-permute-start(bf16[1536,256]{1,0:T(8,128)(2,1)S(1)} %get-tuple-element.114.refs_1_), channel_id=1, source_target_pairs={{0,16},{16,32},{32,48},{48,0},{1,17},{17,33},{33,49},{49,1},{2,18}... | collective-permute-start | bytes 2359304 | tf_op jit(solution)/shard_map/ppermute | solution.py:33
  83.4 37.9 %collective-permute-start.24 = (bf16[1536,256]{1,0:T(8,128)(2,1)S(1)}, bf16[1536,256]{1,0:T(8,128)(2,1)}, u32[]{:S(2)}, u32[]{:S(2)}) collective-permute-start(bf16[1536,256]{1,0:T(8,128)(2,1)S(1)} %get-tuple-element.114.refs_1_), channel_id=1, source_target_pairs={{0,48},{16,0},{32,16},{48,32},{1,49},{17,1},{33,17},{49,33},{2,50}... | collective-permute-start | bytes 2359304 | tf_op jit(solution)/shard_map/ppermute | solution.py:33
  92.7 28.7 %collective-permute-start.20 = (bf16[2,4,32,1024]{3,2,1,0:T(8,128)(2,1)S(1)}, bf16[2,4,32,1024]{3,2,1,0:T(8,128)(2,1)S(1)}, u32[]{:S(2)}, u32[]{:S(2)}) collective-permute-start(bf16[2,4,32,1024]{3,2,1,0:T(8,128)(2,1)S(1)} %slice_bitcast_fusion.1), channel_id=1, source_target_pairs={{0,2},{2,4},{4,6},{6,0},{1,3},{3,5},{5,7},{7,1},{8,10},{10,12},{12... | collective-permute-start | bytes 1572872 | tf_op jit(solution)/shard_map/ppermute | solution.py:37
  94.8 26.6 %collective-permute-start.22 = (bf16[2,4,32,1024]{3,2,1,0:T(8,128)(2,1)}, bf16[2,4,32,1024]{3,2,1,0:T(8,128)(2,1)S(1)}, u32[]{:S(2)}, u32[]{:S(2)}) collective-permute-start(bf16[2,4,32,1024]{3,2,1,0:T(8,128)(2,1)} %slice_bitcast_fusion), channel_id=1, source_target_pairs={{0,6},{2,0},{4,2},{6,4},{1,7},{3,1},{5,3},{7,5},{8,14},{10,8},{12,... | collective-permute-start | bytes 1572872 | tf_op jit(solution)/shard_map/ppermute | solution.py:37
  123.5 16.8 %collective-permute-start.28 = (bf16[4,2,32,4096]{3,2,1,0:T(8,128)(2,1)}, bf16[4,2,32,4096]{3,2,1,0:T(8,128)(2,1)S(1)}, u32[]{:S(2)}, u32[]{:S(2)}) collective-permute-start(bf16[4,2,32,4096]{3,2,1,0:T(8,128)(2,1)} %get-tuple-element.102), channel_id=1, source_target_pairs={{0,1},{1,0},{2,3},{3,2},{4,5},{5,4},{6,7},{7,6},{8,9},{9,8},{10,11... | collective-permute-start | bytes 6291464 | tf_op jit(solution)/shard_map/ppermute | solution.py:41
  123.5 16.7 %collective-permute-start.29 = (bf16[2,2,4,32,1024]{4,3,2,1,0:T(8,128)(2,1)}, bf16[2,2,4,32,1024]{4,3,2,1,0:T(8,128)(2,1)S(1)}, u32[]{:S(2)}, u32[]{:S(2)}) collective-permute-start(bf16[2,2,4,32,1024]{4,3,2,1,0:T(8,128)(2,1)} %copy-done.27), channel_id=1, source_target_pairs={{0,1},{1,0},{2,3},{3,2},{4,5},{5,4},{6,7},{7,6},{8,9},{9,8},{10,11... | collective-permute-start | bytes 3145736 | tf_op jit(solution)/shard_map/ppermute | solution.py:41
  124.0 16.2 %collective-permute-start.32 = (bf16[2,2,4,32,1024]{4,3,2,1,0:T(8,128)(2,1)}, bf16[2,2,4,32,1024]{4,3,2,1,0:T(8,128)(2,1)S(1)}, u32[]{:S(2)}, u32[]{:S(2)}) collective-permute-start(bf16[2,2,4,32,1024]{4,3,2,1,0:T(8,128)(2,1)} %copy-done.26), channel_id=1, source_target_pairs={{0,1},{1,0},{2,3},{3,2},{4,5},{5,4},{6,7},{7,6},{8,9},{9,8},{10,11... | collective-permute-start | bytes 3145736 | tf_op jit(solution)/shard_map/ppermute | solution.py:41
  150.9 18.3 %collective-permute-start.34 = (bf16[1248,256]{1,0:T(8,128)(2,1)}, bf16[1248,256]{1,0:T(8,128)(2,1)S(1)}, u32[]{:S(2)}, u32[]{:S(2)}) collective-permute-start(bf16[1248,256]{1,0:T(8,128)(2,1)} %copy-done.5), channel_id=1, source_target_pairs={{0,16},{16,32},{32,48},{48,0},{1,17},{17,33},{33,49},{49,1},{2,18}... | collective-permute-start | bytes 1916936 | tf_op jit(solution)/shard_map/ppermute | solution.py:33
  152.2 17.1 %collective-permute-start.35 = (bf16[1248,256]{1,0:T(8,128)(2,1)}, bf16[1248,256]{1,0:T(8,128)(2,1)S(1)}, u32[]{:S(2)}, u32[]{:S(2)}) collective-permute-start(bf16[1248,256]{1,0:T(8,128)(2,1)} %copy-done.5), channel_id=1, source_target_pairs={{0,48},{16,0},{32,16},{48,32},{1,49},{17,1},{33,17},{49,33},{2,50}... | collective-permute-start | bytes 1916936 | tf_op jit(solution)/shard_map/ppermute | solution.py:33
  154.4 22.6 %collective-permute-start.38 = (bf16[768,512]{1,0:T(8,128)(2,1)}, bf16[768,512]{1,0:T(8,128)(2,1)}, u32[]{:S(2)}, u32[]{:S(2)}) collective-permute-start(bf16[768,512]{1,0:T(8,128)(2,1)} %copy-done.25), channel_id=1, source_target_pairs={{0,64},{64,0},{1,65},{65,1},{2,66},{66,2},{3,67},{67,3},{4,68},{68... | collective-permute-start | bytes 2359304 | tf_op jit(solution)/shard_map/ppermute | solution.py:41
  174.0 24.5 %collective-permute-start.39 = (bf16[768,512]{1,0:T(8,128)(2,1)}, bf16[768,512]{1,0:T(8,128)(2,1)}, u32[]{:S(2)}, u32[]{:S(2)}) collective-permute-start(bf16[768,512]{1,0:T(8,128)(2,1)} %get-tuple-element.122), channel_id=1, source_target_pairs={{0,64},{64,0},{1,65},{65,1},{2,66},{66,2},{3,67},{67,3},{4,68},{68... | collective-permute-start | bytes 2359304 | tf_op jit(solution)/shard_map/ppermute | solution.py:41
  193.1 22.1 %collective-permute-start.40 = (bf16[768,512]{1,0:T(8,128)(2,1)S(1)}, bf16[768,512]{1,0:T(8,128)(2,1)S(1)}, u32[]{:S(2)}, u32[]{:S(2)}) collective-permute-start(bf16[768,512]{1,0:T(8,128)(2,1)S(1)} %get-tuple-element.125), channel_id=1, source_target_pairs={{0,64},{64,0},{1,65},{65,1},{2,66},{66,2},{3,67},{67,3},{4,68},{68... | collective-permute-start | bytes 2359304 | tf_op jit(solution)/shard_map/ppermute | solution.py:41
  204.3 19.4 %collective-permute-start.41 = (bf16[480,512]{1,0:T(8,128)(2,1)S(1)}, bf16[480,512]{1,0:T(8,128)(2,1)S(1)}, u32[]{:S(2)}, u32[]{:S(2)}) collective-permute-start(bf16[480,512]{1,0:T(8,128)(2,1)S(1)} %get-tuple-element.131), channel_id=1, source_target_pairs={{0,64},{64,0},{1,65},{65,1},{2,66},{66,2},{3,67},{67,3},{4,68},{68... | collective-permute-start | bytes 1474568 | tf_op jit(solution)/shard_map/ppermute | solution.py:41
  (60 other events, 384.8 us)
Sparse Core Ops, SparseCore 0:
  47.6 75.8 all-gather.1
  151.0 31.5 reduce-scatter.1

commit v2 on v1

--- a/solution.py
+++ b/solution.py
@@ -260,9 +260,9 @@
     batch0 = [mine, left, right, partner]
     batch0 += core_swaps(batch0)
     both = ((None, 0),), ((None, 1),), ((None, 2),), ((None, 3),)
-    own0, dn0 = hidden_call(batch0, both, ((0, 1, 2, 3),), wg_rows, wu_rows, w_down)
-    own0, dn0, p_right, p_left, shares, other_shares = gate(own0, dn0, p_right, p_left, shares, other_shares)
-    gathered0 = lax.all_gather(own0, "x", axis=0, tiled=True)
+    *own0, dn0 = hidden_call(batch0, both, ((0, 1), (2, 3)), wg_rows, wu_rows, w_down)
+    *own0, dn0, p_right, p_left, shares, other_shares = gate(*own0, dn0, p_right, p_left, shares, other_shares)
+    gathered0 = [lax.all_gather(own0[0], "x", axis=0, tiled=True)]
 
     far_in = send_z(jnp.stack([right[0], p_right[0]]), 1)
     far_grad = send_z(jnp.stack([left[1], p_left[1]]), -1)
@@ -279,44 +279,47 @@
     c_far_in, c_far_grad = send_z(c_right[:, 0], 1), send_z(c_left[:, 1], -1)
     shares_other = swap(shares, "core")
     term_own, term_other = in_grads_call(pos, dn0, dn1, wg_rows, wu_rows)
-    term_own, term_other, c_far_in, c_far_grad, right1[0], left1[0], own1[1], shares_other, c_left, c_right, gathered0 = gate(
-        term_own, term_other, c_far_in, c_far_grad, right1[0], left1[0], own1[1], shares_other, c_left, c_right, gathered0
+    term_own, term_other, c_far_in, c_far_grad, right1[0], left1[0], own1[1], shares_other, c_left, c_right, gathered0[0] = gate(
+        term_own, term_other, c_far_in, c_far_grad, right1[0], left1[0], own1[1], shares_other, c_left, c_right, gathered0[0]
     )
 
     far1 = [send_x(right1[0][:cut], 1), send_x(left1[0][cut:], -1)]
     c_here = [c_left, c_far_in, c_far_grad, c_right]
     c_other = core_swaps(c_here)
     term_other = swap(term_other, "core")
-    *far1, own1[1], term_other = gate(*far1, own1[1], term_other, *c_other)[:4]
+    *far1, own1[1], own0[1], term_other = gate(*far1, own1[1], own0[1], term_other, *c_other)[:5]
+    gathered0.append(lax.all_gather(own0[1], "x", axis=0, tiled=True))
     col_pieces = [shares, *c_here, shares_other, *c_other]
     kept, sent, got = [], [], []
 
     def weights(j):
         side, start = j // 2, cut * (j % 2)
-        pieces = [gathered0, own1[side], right1[side], left1[side], far1[j]]
-        send, keep = weights_call(UNITS[j], pos, (cut * j, own0.shape[0], start), pieces, col_pieces)
+        pieces = [gathered0[side], own1[side], right1[side], left1[side], far1[j]]
+        send, keep = weights_call(UNITS[j], pos, (start, own0[side].shape[0], start), pieces, col_pieces)
         kept.append(keep)
         sent.append(send)
 
     right1.append(send_x(own1[1], 1))
     left1.append(send_x(own1[1], -1))
     weights(0)
-    sent[0], own1[0], term_other = gate(sent[0], own1[0], term_other)
-    pair = (term_own.astype(F32) + term_other.astype(F32)).astype(BF)
-    scattered = lax.psum_scatter(pair.reshape(256, D), "z", scatter_dimension=0, tiled=True)
+    sent[0], own1[0] = gate(sent[0], own1[0])
     got.append(swap(sent[0], "yh"))
     weights(1)
-    right1[1], left1[1], sent[1] = gate(right1[1], left1[1], sent[1])
+    pair = (term_own.astype(F32) + term_other.astype(F32)).astype(BF)
+    right1[1], left1[1], _, gathered0[1], pair, got[0] = gate(
+        right1[1], left1[1], sent[1], gathered0[1], pair, got[0]
+    )
+    scattered = lax.psum_scatter(pair.reshape(256, D), "z", scatter_dimension=0, tiled=True)
     got.append(swap(sent[1], "yh"))
     far1 += [send_x(right1[1][:cut], 1), send_x(left1[1][cut:], -1)]
     scattered = scattered.reshape(2, 32, D)
     mine_part = lax.dynamic_index_in_dim(scattered, yl, axis=0, keepdims=False)
     other_part = lax.dynamic_index_in_dim(scattered, 1 - yl, axis=0, keepdims=False)
     in_grads = (mine_part.astype(F32) + swap(other_part, "yl").astype(F32)).astype(BF)
-    far1[2], far1[3], got[0], own1[1] = gate(far1[2], far1[3], got[0], own1[1])
+    far1[2], far1[3], got[1], own1[1] = gate(far1[2], far1[3], got[1], own1[1])
     weights(2)
     got.append(swap(sent[2], "yh"))
-    got[1], sent[2], own1[1] = gate(got[1], sent[2], own1[1])
+    sent[2], own1[1] = gate(sent[2], own1[1])
     weights(3)
     got.append(swap(sent[3], "yh"))
     sent = got

time: 240 us -> 248 us (1.033)
  waiting for transfers between devices: 73.6 us -> 83.6 us
  local copies, waits for them, and re-layouts: 22.9 us -> 18.9 us
    ppermute x21, waiting for transfers between devices: 23 us -> 43.5 us  [swap(): return lax.ppermute(a, axis, [(0, 1), (1, 0)])]
    ppermute x11, waiting for transfers between devices: 28.4 us -> 15.7 us  [send_x(): return lax.ppermute(a, 'x', ring(4, step))]
    unnamed x80 -> x64, local copies, waits for them, and re-layouts: 17.2 us -> 13 us
  transfers between devices with their start and end apart: 44 -> 45, of which waited for: 19 -> 15; matrix products, arithmetic and copies ran while one was open for 5% -> 7% of each run, Pallas kernels for 25% -> 27%
where the time goes in v2:
time: 248 us; the launch traced here: 247 us
  waiting for transfers between devices  83.6 us (34%)
  Pallas kernels  67.9 us (27%)
  starting transfers between devices  48.8 us (20%)
  local copies, waits for them, and re-layouts  18.9 us (8%)
  between operations  14.2 us (6%)
  other arithmetic  13.9 us (6%)
    ppermute x21, waiting for transfers between devices, swap(): return lax.ppermute(a, axis, [(0, 1), (1, 0)])  43.5 us
    pallas_call x4, Pallas kernels, weights_call(): pl.pallas_call(functools.partial(weights_kernel, n, places), in_specs=[pl...  27.4 us
    pallas_call x2, Pallas kernels, hidden_call(): pl.pallas_call(functools.partial(hidden_kernel, places, outs), grid=(N_TI...  26.3 us
    ppermute x10, waiting for transfers between devices, send_z(): return lax.ppermute(a, 'z', ring(4, step))  19.8 us
    ppermute x11, starting transfers between devices, send_x(): return lax.ppermute(a, 'x', ring(4, step))  18.5 us
    ppermute x11, waiting for transfers between devices, send_x(): return lax.ppermute(a, 'x', ring(4, step))  15.7 us
    ppermute x10, starting transfers between devices, send_z(): return lax.ppermute(a, 'z', ring(4, step))  15.2 us
    ppermute x21, starting transfers between devices, swap(): return lax.ppermute(a, axis, [(0, 1), (1, 0)])  15 us
  transfers between devices with their start and end apart: 45, of which 15 were waited for; matrix products, arithmetic and copies ran while one was open for 7% of the time, Pallas kernels for 27%

profile of v2, /device:TPU:0, one launch (start us, length us, event | category | flops | bytes accessed | tf_op | source)
XLA Modules:
  0.0 247.5 jit_solution(18130280637811244025)
XLA Ops:
  23.4 4.5 %collective-permute-done.5 = bf16[2,32,1024]{2,1,0:T(8,128)(2,1)S(1)} collective-permute-done((bf16[2,32,1024]{2,1,0:T(8,128)(2,1)S(1)}, bf16[2,32,1024]{2,1,0:T(8,128)(2,1)S(1)}, u32[]{:S(2)}, u32[]{:S(2)}) %collective-permute-start.5) | collective-permute-done | bytes 131104 | tf_op jit(solution)/shard_map/ppermute | solution.py:33
  32.4 13.2 %hidden_grads.2 = (bf16[1536,256]{1,0:T(8,128)(2,1)}, bf16[1248,256]{1,0:T(8,128)(2,1)S(1)}, bf16[2,256,924]{2,1,0:T(8,128)(2,1)}) custom-call(bf16[2,32,4096]{2,1,0:T(8,128)(2,1)S(1)} %pad_maximum_fusion.refs_0_, bf16[2,32,4096]{2,1,0:T(8,128)(2,1)S(1)} %collective-permute-done.1.refs_1_, bf16[2,32,4096]{2,1,0:T(8,128)(2,1)S(1)} %collective-permute-done.refs_2_, ...), custom_call_target="tpu_custom_call" | custom-call | flops 726663168 | bytes 2838528 | tf_op jit(solution)/shard_map/hidden_grads/pallas_call | solution.py:104
  50.2 11.1 %collective-permute-done.14.refs_1_ = bf16[2,32,4096]{2,1,0:T(8,128)(2,1)S(1)} collective-permute-done((bf16[2,32,4096]{2,1,0:T(8,128)(2,1)S(1)}, bf16[2,32,4096]{2,1,0:T(8,128)(2,1)S(1)}, u32[]{:S(2)}, u32[]{:S(2)}) %collective-permute-start.14) | collective-permute-done | bytes 524320 | tf_op jit(solution)/shard_map/ppermute | solution.py:37
  65.8 3.2 %collective-permute-start.21 = (bf16[2,2,4,32,1024]{4,3,2,1,0:T(8,128)(2,1)}, bf16[2,2,4,32,1024]{4,3,2,1,0:T(8,128)(2,1)S(1)}, u32[]{:S(2)}, u32[]{:S(2)}) collective-permute-start(bf16[2,2,4,32,1024]{4,3,2,1,0:T(8,128)(2,1)} %pad_maximum_fusion.1.refs_5_), channel_id=1, source_target_pairs={{0,6},{2,0},{4,2},{6,4},{1,7},{3,1},{5,3},{7,5},{8,14},{10,8},{12,... | collective-permute-start | bytes 3145736 | tf_op jit(solution)/shard_map/ppermute | solution.py:37
  69.0 13.1 %hidden_grads.3 = (bf16[1536,256]{1,0:T(8,128)(2,1)S(1)}, bf16[1248,256]{1,0:T(8,128)(2,1)S(1)}, bf16[2,256,924]{2,1,0:T(8,128)(2,1)}) custom-call(bf16[2,32,4096]{2,1,0:T(8,128)(2,1)S(1)} %collective-permute-done.13.refs_0_, bf16[2,32,4096]{2,1,0:T(8,128)(2,1)S(1)} %collective-permute-done.14.refs_1_, bf16[2,32,4096]{2,1,0:T(8,128)(2,1)S(1)} %copy-done.7, ...), custom_call_target="tpu_custom_call" | custom-call | flops 726663168 | bytes 2838528 | tf_op jit(solution)/shard_map/hidden_grads/pallas_call | solution.py:104
  83.2 3.0 %collective-permute-start.24 = (bf16[1536,256]{1,0:T(8,128)(2,1)S(1)}, bf16[1536,256]{1,0:T(8,128)(2,1)}, u32[]{:S(2)}, u32[]{:S(2)}) collective-permute-start(bf16[1536,256]{1,0:T(8,128)(2,1)S(1)} %get-tuple-element.115.refs_1_), channel_id=1, source_target_pairs={{0,48},{16,0},{32,16},{48,32},{1,49},{17,1},{33,17},{49,33},{2,50}... | collective-permute-start | bytes 2359304 | tf_op jit(solution)/shard_map/ppermute | solution.py:33
  86.2 6.2 %collective-permute-done.19.refs_9_ = bf16[2,2,4,32,1024]{4,3,2,1,0:T(8,128)(2,1)S(1)} collective-permute-done((bf16[2,2,4,32,1024]{4,3,2,1,0:T(8,128)(2,1)}, bf16[2,2,4,32,1024]{4,3,2,1,0:T(8,128)(2,1)S(1)}, u32[]{:S(2)}, u32[]{:S(2)}) %collective-permute-start.19) | collective-permute-done | bytes 1048608 | tf_op jit(solution)/shard_map/ppermute | solution.py:37
  95.3 3.0 %collective-permute-start.22 = (bf16[2,4,32,1024]{3,2,1,0:T(8,128)(2,1)}, bf16[2,4,32,1024]{3,2,1,0:T(8,128)(2,1)S(1)}, u32[]{:S(2)}, u32[]{:S(2)}) collective-permute-start(bf16[2,4,32,1024]{3,2,1,0:T(8,128)(2,1)} %slice_bitcast_fusion), channel_id=1, source_target_pairs={{0,6},{2,0},{4,2},{6,4},{1,7},{3,1},{5,3},{7,5},{8,14},{10,8},{12,... | collective-permute-start | bytes 1572872 | tf_op jit(solution)/shard_map/ppermute | solution.py:37
  100.9 14.2 %in_grads_terms.1 = (bf16[4,2,32,4096]{3,2,1,0:T(8,128)(2,1)S(1)}, bf16[4,2,32,4096]{3,2,1,0:T(8,128)(2,1)}) custom-call(s32[3]{0:T(128)S(1)} %pad_add_fusion.pos_ref, bf16[2,256,924]{2,1,0:T(8,128)(2,1)S(1)} %copy-done.8, bf16[2,256,924]{2,1,0:T(8,128)(2,1)S(1)} %copy-done.9, bf16[924,4096]{1,0:T(8,128)(2,1)} %bitcast.36, bf16[924,4096]{1,0:T(8,128)(2,1)} %bitcast.39), custom_call_target="tpu_custom_call" | custom-call | flops 968884224 | bytes 1892352 | tf_op jit(solution)/shard_map/in_grads_terms/pallas_call | solution.py:146
  118.6 3.0 %collective-permute-start.27 = (bf16[768,256]{1,0:T(8,128)(2,1)S(1)}, bf16[768,256]{1,0:T(8,128)(2,1)S(1)}, u32[]{:S(2)}, u32[]{:S(2)}) collective-permute-start(bf16[768,256]{1,0:T(8,128)(2,1)S(1)} %slice.73), channel_id=1, source_target_pairs={{0,48},{16,0},{32,16},{48,32},{1,49},{17,1},{33,17},{49,33},{2,50}... | collective-permute-start | bytes 1179656 | tf_op jit(solution)/shard_map/ppermute | solution.py:33
  121.6 8.3 %collective-permute-done.26.refs_4_ = bf16[768,256]{1,0:T(8,128)(2,1)S(1)} collective-permute-done((bf16[768,256]{1,0:T(8,128)(2,1)S(1)}, bf16[768,256]{1,0:T(8,128)(2,1)S(1)}, u32[]{:S(2)}, u32[]{:S(2)}) %collective-permute-start.26) | collective-permute-done | bytes 393248 | tf_op jit(solution)/shard_map/ppermute | solution.py:33
  139.0 7.4 %weight_grads.4 = (bf16[768,512]{1,0:T(8,128)(2,1)S(1)}, bf16[768,512]{1,0:T(8,128)(2,1)S(1)}) custom-call(s32[3]{0:T(128)S(1)} %pad_add_fusion.pos_ref, bf16[6144,256]{1,0:T(8,128)(2,1)} %all-gather.3.cloned.1.call-done.refs_0_, bf16[1536,256]{1,0:T(8,128)(2,1)S(1)} %copy-done.1, bf16[1536,256]{1,0:T(8,128)(2,1)S(1)} %collective-permute-done.23.refs_2_, ...), custom_call_target="tpu_custom_call" | custom-call | flops 402653184 | bytes 1572864 | tf_op jit(solution)/shard_map/weight_grads/pallas_call | solution.py:215
  147.3 2.8 %collective-permute-start.35 = (bf16[768,512]{1,0:T(8,128)(2,1)S(1)}, bf16[768,512]{1,0:T(8,128)(2,1)}, u32[]{:S(2)}, u32[]{:S(2)}) collective-permute-start(bf16[768,512]{1,0:T(8,128)(2,1)S(1)} %get-tuple-element.121), channel_id=1, source_target_pairs={{0,64},{64,0},{1,65},{65,1},{2,66},{66,2},{3,67},{67,3},{4,68},{68... | collective-permute-start | bytes 2359304 | tf_op jit(solution)/shard_map/ppermute | solution.py:41
  151.1 7.1 %weight_grads.5 = (bf16[768,512]{1,0:T(8,128)(2,1)S(1)}, bf16[768,512]{1,0:T(8,128)(2,1)S(1)}) custom-call(s32[3]{0:T(128)S(1)} %pad_add_fusion.pos_ref, bf16[6144,256]{1,0:T(8,128)(2,1)} %all-gather.3.cloned.1.call-done.refs_0_, bf16[1536,256]{1,0:T(8,128)(2,1)S(1)} %copy-done.1, bf16[1536,256]{1,0:T(8,128)(2,1)S(1)} %collective-permute-done.23.refs_2_, ...), custom_call_target="tpu_custom_call" | custom-call | flops 402653184 | bytes 1572864 | tf_op jit(solution)/shard_map/weight_grads/pallas_call | solution.py:215
  158.2 4.3 %add_convert_fusion = bf16[4,2,32,4096]{3,2,1,0:T(8,128)(2,1)} fusion(bf16[4,2,32,4096]{3,2,1,0:T(8,128)(2,1)} %collective-permute-done.28, bf16[4,2,32,4096]{3,2,1,0:T(8,128)(2,1)S(1)} %copy-done.5), kind=kLoop, calls=%fused_computation | loop fusion | flops 4194304 | bytes 6291456 | tf_op jit(solution)/shard_map/convert_element_type | solution.py:308
  162.5 5.6 %collective-permute-done.35 = bf16[768,512]{1,0:T(8,128)(2,1)} collective-permute-done((bf16[768,512]{1,0:T(8,128)(2,1)S(1)}, bf16[768,512]{1,0:T(8,128)(2,1)}, u32[]{:S(2)}, u32[]{:S(2)}) %collective-permute-start.35) | collective-permute-done | bytes 786464 | tf_op jit(solution)/shard_map/ppermute | solution.py:41
  168.1 4.5 %all-gather.5.cloned.1.call-done.refs_0_ = bf16[4992,256]{1,0:T(8,128)(2,1)} async-done(((bf16[1248,256]{1,0:T(8,128)(2,1)}), bf16[4992,256]{1,0:T(8,128)(2,1)}) %all-gather.5.cloned.1.call-update) | async-done | bytes 2555920 | tf_op jit(solution)/shard_map/all_gather | solution.py:291
  172.7 3.0 %collective-permute-start.39 = (bf16[768,512]{1,0:T(8,128)(2,1)}, bf16[768,512]{1,0:T(8,128)(2,1)}, u32[]{:S(2)}, u32[]{:S(2)}) collective-permute-start(bf16[768,512]{1,0:T(8,128)(2,1)} %copy-done.19), channel_id=1, source_target_pairs={{0,64},{64,0},{1,65},{65,1},{2,66},{66,2},{3,67},{67,3},{4,68},{68... | collective-permute-start | bytes 2359304 | tf_op jit(solution)/shard_map/ppermute | solution.py:41
  182.3 11.7 %collective-permute-done.39 = bf16[768,512]{1,0:T(8,128)(2,1)} collective-permute-done((bf16[768,512]{1,0:T(8,128)(2,1)}, bf16[768,512]{1,0:T(8,128)(2,1)}, u32[]{:S(2)}, u32[]{:S(2)}) %collective-permute-start.39) | collective-permute-done | bytes 786464 | tf_op jit(solution)/shard_map/ppermute | solution.py:41
  194.1 7.2 %weight_grads.6 = (bf16[768,512]{1,0:T(8,128)(2,1)S(1)}, bf16[768,512]{1,0:T(8,128)(2,1)S(1)}) custom-call(s32[3]{0:T(128)S(1)} %pad_add_fusion.pos_ref, bf16[4992,256]{1,0:T(8,128)(2,1)} %all-gather.5.cloned.1.call-done.refs_0_, bf16[1248,256]{1,0:T(8,128)(2,1)S(1)} %copy-done.3, bf16[1248,256]{1,0:T(8,128)(2,1)S(1)} %collective-permute-done.33.refs_2_, ...), custom_call_target="tpu_custom_call" | custom-call | flops 402653184 | bytes 1572864 | tf_op jit(solution)/shard_map/weight_grads/pallas_call | solution.py:215
  201.3 3.0 %collective-permute-start.40 = (bf16[768,512]{1,0:T(8,128)(2,1)S(1)}, bf16[768,512]{1,0:T(8,128)(2,1)S(1)}, u32[]{:S(2)}, u32[]{:S(2)}) collective-permute-start(bf16[768,512]{1,0:T(8,128)(2,1)S(1)} %get-tuple-element.133), channel_id=1, source_target_pairs={{0,64},{64,0},{1,65},{65,1},{2,66},{66,2},{3,67},{67,3},{4,68},{68... | collective-permute-start | bytes 2359304 | tf_op jit(solution)/shard_map/ppermute | solution.py:41
  204.2 5.8 %weight_grads.7 = (bf16[480,512]{1,0:T(8,128)(2,1)S(1)}, bf16[480,512]{1,0:T(8,128)(2,1)S(1)}) custom-call(s32[3]{0:T(128)S(1)} %pad_add_fusion.pos_ref, bf16[4992,256]{1,0:T(8,128)(2,1)} %all-gather.5.cloned.1.call-done.refs_0_, bf16[1248,256]{1,0:T(8,128)(2,1)S(1)} %copy-done.3, bf16[1248,256]{1,0:T(8,128)(2,1)S(1)} %collective-permute-done.33.refs_2_, ...), custom_call_target="tpu_custom_call" | custom-call | flops 251658240 | bytes 1572864 | tf_op jit(solution)/shard_map/weight_grads/pallas_call | solution.py:215
  212.2 19.8 %collective-permute-done.41 = bf16[480,512]{1,0:T(8,128)(2,1)S(1)} collective-permute-done((bf16[480,512]{1,0:T(8,128)(2,1)S(1)}, bf16[480,512]{1,0:T(8,128)(2,1)S(1)}, u32[]{:S(2)}, u32[]{:S(2)}) %collective-permute-start.41) | collective-permute-done | bytes 491552 | tf_op jit(solution)/shard_map/ppermute | solution.py:41
  236.9 3.3 %collective-permute-done.36 = bf16[32,4096]{1,0:T(8,128)(2,1)S(1)} collective-permute-done((bf16[32,4096]{1,0:T(8,128)(2,1)S(1)}, bf16[32,4096]{1,0:T(8,128)(2,1)S(1)}, u32[]{:S(2)}, u32[]{:S(2)}) %collective-permute-start.36) | collective-permute-done | bytes 262176 | tf_op jit(solution)/shard_map/ppermute | solution.py:41
  (175 shorter events, 64.9 us)
Async XLA Ops:
  7.2 109.3 %all-gather.3.cloned.1.call-start = ((), (), s32[]{:S(2)}) async-start(), calls=%async_computation.1 | async-start | bytes 3932160 | tf_op jit(solution)/shard_map/all_gather | solution.py:265
  8.4 19.6 %collective-permute-start = (bf16[2,32,4096]{2,1,0:T(8,128)(2,1)S(1)}, bf16[2,32,4096]{2,1,0:T(8,128)(2,1)S(1)}, u32[]{:S(2)}, u32[]{:S(2)}) collective-permute-start(bf16[2,32,4096]{2,1,0:T(8,128)(2,1)S(1)} %pad_maximum_fusion.refs_0_), channel_id=1, source_target_pairs={{0,2},{2,4},{4,6},{6,0},{1,3},{3,5},{5,7},{7,1},{8,10},{10,12},{12... | collective-permute-start | bytes 1572872 | tf_op jit(solution)/shard_map/ppermute | solution.py:37
  10.4 17.5 %collective-permute-start.1 = (bf16[2,32,4096]{2,1,0:T(8,128)(2,1)S(1)}, bf16[2,32,4096]{2,1,0:T(8,128)(2,1)S(1)}, u32[]{:S(2)}, u32[]{:S(2)}) collective-permute-start(bf16[2,32,4096]{2,1,0:T(8,128)(2,1)S(1)} %pad_maximum_fusion.refs_0_), channel_id=1, source_target_pairs={{0,6},{2,0},{4,2},{6,4},{1,7},{3,1},{5,3},{7,5},{8,14},{10,8},{12,... | collective-permute-start | bytes 1572872 | tf_op jit(solution)/shard_map/ppermute | solution.py:37
  28.5 17.9 %collective-permute-start.10 = (bf16[2,32,4096]{2,1,0:T(8,128)(2,1)S(1)}, bf16[2,32,4096]{2,1,0:T(8,128)(2,1)S(1)}, u32[]{:S(2)}, u32[]{:S(2)}) collective-permute-start(bf16[2,32,4096]{2,1,0:T(8,128)(2,1)S(1)} %collective-permute-done.2.refs_3_), channel_id=1, source_target_pairs={{0,2},{2,4},{4,6},{6,0},{1,3},{3,5},{5,7},{7,1},{8,10},{10,12},{12... | collective-permute-start | bytes 1572872 | tf_op jit(solution)/shard_map/ppermute | solution.py:37
  28.7 17.7 %collective-permute-start.12 = (bf16[2,4,32,1024]{3,2,1,0:T(8,128)(2,1)S(1)}, bf16[2,4,32,1024]{3,2,1,0:T(8,128)(2,1)S(1)}, u32[]{:S(2)}, u32[]{:S(2)}) collective-permute-start(bf16[2,4,32,1024]{3,2,1,0:T(8,128)(2,1)S(1)} %pad_maximum_fusion.3), channel_id=1, source_target_pairs={{0,8},{8,0},{1,9},{9,1},{2,10},{10,2},{3,11},{11,3},{4,12},{12,4},... | collective-permute-start | bytes 1572872 | tf_op jit(solution)/shard_map/ppermute | solution.py:41
  29.9 16.5 %collective-permute-start.11 = (bf16[2,32,4096]{2,1,0:T(8,128)(2,1)S(1)}, bf16[2,32,4096]{2,1,0:T(8,128)(2,1)S(1)}, u32[]{:S(2)}, u32[]{:S(2)}) collective-permute-start(bf16[2,32,4096]{2,1,0:T(8,128)(2,1)S(1)} %collective-permute-done.2.refs_3_), channel_id=1, source_target_pairs={{0,6},{2,0},{4,2},{6,4},{1,7},{3,1},{5,3},{7,5},{8,14},{10,8},{12,... | collective-permute-start | bytes 1572872 | tf_op jit(solution)/shard_map/ppermute | solution.py:37
  47.3 125.4 %all-gather.5.cloned.1.call-start = ((), (), s32[]{:S(2)}) async-start(), calls=%async_computation.2 | async-start | bytes 3194880 | tf_op jit(solution)/shard_map/all_gather | solution.py:291
  65.8 26.6 %collective-permute-start.19 = (bf16[2,2,4,32,1024]{4,3,2,1,0:T(8,128)(2,1)}, bf16[2,2,4,32,1024]{4,3,2,1,0:T(8,128)(2,1)S(1)}, u32[]{:S(2)}, u32[]{:S(2)}) collective-permute-start(bf16[2,2,4,32,1024]{4,3,2,1,0:T(8,128)(2,1)} %pad_maximum_fusion.1.refs_5_), channel_id=1, source_target_pairs={{0,2},{2,4},{4,6},{6,0},{1,3},{3,5},{5,7},{7,1},{8,10},{10,12},{12... | collective-permute-start | bytes 3145736 | tf_op jit(solution)/shard_map/ppermute | solution.py:37
  65.8 27.6 %collective-permute-start.21 = (bf16[2,2,4,32,1024]{4,3,2,1,0:T(8,128)(2,1)}, bf16[2,2,4,32,1024]{4,3,2,1,0:T(8,128)(2,1)S(1)}, u32[]{:S(2)}, u32[]{:S(2)}) collective-permute-start(bf16[2,2,4,32,1024]{4,3,2,1,0:T(8,128)(2,1)} %pad_maximum_fusion.1.refs_5_), channel_id=1, source_target_pairs={{0,6},{2,0},{4,2},{6,4},{1,7},{3,1},{5,3},{7,5},{8,14},{10,8},{12,... | collective-permute-start | bytes 3145736 | tf_op jit(solution)/shard_map/ppermute | solution.py:37
  69.0 47.4 %collective-permute-start.25 = (bf16[2,2,4,32,1024]{4,3,2,1,0:T(8,128)(2,1)}, bf16[2,2,4,32,1024]{4,3,2,1,0:T(8,128)(2,1)}, u32[]{:S(2)}, u32[]{:S(2)}) collective-permute-start(bf16[2,2,4,32,1024]{4,3,2,1,0:T(8,128)(2,1)} %pad_maximum_fusion.1.refs_5_), channel_id=1, source_target_pairs={{0,1},{1,0},{2,3},{3,2},{4,5},{5,4},{6,7},{7,6},{8,9},{9,8},{10,11... | collective-permute-start | bytes 3145736 | tf_op jit(solution)/shard_map/ppermute | solution.py:41
  83.0 33.4 %collective-permute-start.23 = (bf16[1536,256]{1,0:T(8,128)(2,1)S(1)}, bf16[1536,256]{1,0:T(8,128)(2,1)S(1)}, u32[]{:S(2)}, u32[]{:S(2)}) collective-permute-start(bf16[1536,256]{1,0:T(8,128)(2,1)S(1)} %get-tuple-element.115.refs_1_), channel_id=1, source_target_pairs={{0,16},{16,32},{32,48},{48,0},{1,17},{17,33},{33,49},{49,1},{2,18}... | collective-permute-start | bytes 2359304 | tf_op jit(solution)/shard_map/ppermute | solution.py:33
  83.2 33.2 %collective-permute-start.24 = (bf16[1536,256]{1,0:T(8,128)(2,1)S(1)}, bf16[1536,256]{1,0:T(8,128)(2,1)}, u32[]{:S(2)}, u32[]{:S(2)}) collective-permute-start(bf16[1536,256]{1,0:T(8,128)(2,1)S(1)} %get-tuple-element.115.refs_1_), channel_id=1, source_target_pairs={{0,48},{16,0},{32,16},{48,32},{1,49},{17,1},{33,17},{49,33},{2,50}... | collective-permute-start | bytes 2359304 | tf_op jit(solution)/shard_map/ppermute | solution.py:33
  93.3 23.1 %collective-permute-start.20 = (bf16[2,4,32,1024]{3,2,1,0:T(8,128)(2,1)}, bf16[2,4,32,1024]{3,2,1,0:T(8,128)(2,1)S(1)}, u32[]{:S(2)}, u32[]{:S(2)}) collective-permute-start(bf16[2,4,32,1024]{3,2,1,0:T(8,128)(2,1)} %slice_bitcast_fusion.1), channel_id=1, source_target_pairs={{0,2},{2,4},{4,6},{6,0},{1,3},{3,5},{5,7},{7,1},{8,10},{10,12},{12... | collective-permute-start | bytes 1572872 | tf_op jit(solution)/shard_map/ppermute | solution.py:37
  95.3 21.1 %collective-permute-start.22 = (bf16[2,4,32,1024]{3,2,1,0:T(8,128)(2,1)}, bf16[2,4,32,1024]{3,2,1,0:T(8,128)(2,1)S(1)}, u32[]{:S(2)}, u32[]{:S(2)}) collective-permute-start(bf16[2,4,32,1024]{3,2,1,0:T(8,128)(2,1)} %slice_bitcast_fusion), channel_id=1, source_target_pairs={{0,6},{2,0},{4,2},{6,4},{1,7},{3,1},{5,3},{7,5},{8,14},{10,8},{12,... | collective-permute-start | bytes 1572872 | tf_op jit(solution)/shard_map/ppermute | solution.py:37
  116.5 17.0 %collective-permute-start.28 = (bf16[4,2,32,4096]{3,2,1,0:T(8,128)(2,1)}, bf16[4,2,32,4096]{3,2,1,0:T(8,128)(2,1)}, u32[]{:S(2)}, u32[]{:S(2)}) collective-permute-start(bf16[4,2,32,4096]{3,2,1,0:T(8,128)(2,1)} %get-tuple-element.105), channel_id=1, source_target_pairs={{0,1},{1,0},{2,3},{3,2},{4,5},{5,4},{6,7},{7,6},{8,9},{9,8},{10,11... | collective-permute-start | bytes 6291464 | tf_op jit(solution)/shard_map/ppermute | solution.py:41
  116.6 16.9 %collective-permute-start.29 = (bf16[2,2,4,32,1024]{4,3,2,1,0:T(8,128)(2,1)}, bf16[2,2,4,32,1024]{4,3,2,1,0:T(8,128)(2,1)}, u32[]{:S(2)}, u32[]{:S(2)}) collective-permute-start(bf16[2,2,4,32,1024]{4,3,2,1,0:T(8,128)(2,1)} %copy-done.21), channel_id=1, source_target_pairs={{0,1},{1,0},{2,3},{3,2},{4,5},{5,4},{6,7},{7,6},{8,9},{9,8},{10,11... | collective-permute-start | bytes 3145736 | tf_op jit(solution)/shard_map/ppermute | solution.py:41
  133.5 99.1 %reduce-scatter.2.cloned.1.call-start = ((), (), s32[]{:S(2)}) async-start(), calls=%async_computation.3 | async-start | bytes 2621440 | tf_op jit(solution)/shard_map/reduce_scatter | solution.py:312
  133.5 29.0 %collective-permute-start.33 = (bf16[1248,256]{1,0:T(8,128)(2,1)}, bf16[1248,256]{1,0:T(8,128)(2,1)S(1)}, u32[]{:S(2)}, u32[]{:S(2)}) collective-permute-start(bf16[1248,256]{1,0:T(8,128)(2,1)} %copy-done.2), channel_id=1, source_target_pairs={{0,16},{16,32},{32,48},{48,0},{1,17},{17,33},{33,49},{49,1},{2,18}... | collective-permute-start | bytes 1916936 | tf_op jit(solution)/shard_map/ppermute | solution.py:33
  134.1 28.4 %collective-permute-start.34 = (bf16[1248,256]{1,0:T(8,128)(2,1)}, bf16[1248,256]{1,0:T(8,128)(2,1)}, u32[]{:S(2)}, u32[]{:S(2)}) collective-permute-start(bf16[1248,256]{1,0:T(8,128)(2,1)} %copy-done.2), channel_id=1, source_target_pairs={{0,48},{16,0},{32,16},{48,32},{1,49},{17,1},{33,17},{49,33},{2,50}... | collective-permute-start | bytes 1916936 | tf_op jit(solution)/shard_map/ppermute | solution.py:33
  147.3 20.9 %collective-permute-start.35 = (bf16[768,512]{1,0:T(8,128)(2,1)S(1)}, bf16[768,512]{1,0:T(8,128)(2,1)}, u32[]{:S(2)}, u32[]{:S(2)}) collective-permute-start(bf16[768,512]{1,0:T(8,128)(2,1)S(1)} %get-tuple-element.121), channel_id=1, source_target_pairs={{0,64},{64,0},{1,65},{65,1},{2,66},{66,2},{3,67},{67,3},{4,68},{68... | collective-permute-start | bytes 2359304 | tf_op jit(solution)/shard_map/ppermute | solution.py:41
  172.7 21.4 %collective-permute-start.39 = (bf16[768,512]{1,0:T(8,128)(2,1)}, bf16[768,512]{1,0:T(8,128)(2,1)}, u32[]{:S(2)}, u32[]{:S(2)}) collective-permute-start(bf16[768,512]{1,0:T(8,128)(2,1)} %copy-done.19), channel_id=1, source_target_pairs={{0,64},{64,0},{1,65},{65,1},{2,66},{66,2},{3,67},{67,3},{4,68},{68... | collective-permute-start | bytes 2359304 | tf_op jit(solution)/shard_map/ppermute | solution.py:41
  175.7 18.4 %collective-permute-start.37 = (bf16[768,256]{1,0:T(8,128)(2,1)S(1)}, bf16[768,256]{1,0:T(8,128)(2,1)S(1)}, u32[]{:S(2)}, u32[]{:S(2)}) collective-permute-start(bf16[768,256]{1,0:T(8,128)(2,1)S(1)} %slice.75), channel_id=1, source_target_pairs={{0,16},{16,32},{32,48},{48,0},{1,17},{17,33},{33,49},{49,1},{2,18}... | collective-permute-start | bytes 1179656 | tf_op jit(solution)/shard_map/ppermute | solution.py:33
  201.3 30.9 %collective-permute-start.40 = (bf16[768,512]{1,0:T(8,128)(2,1)S(1)}, bf16[768,512]{1,0:T(8,128)(2,1)S(1)}, u32[]{:S(2)}, u32[]{:S(2)}) collective-permute-start(bf16[768,512]{1,0:T(8,128)(2,1)S(1)} %get-tuple-element.133), channel_id=1, source_target_pairs={{0,64},{64,0},{1,65},{65,1},{2,66},{66,2},{3,67},{67,3},{4,68},{68... | collective-permute-start | bytes 2359304 | tf_op jit(solution)/shard_map/ppermute | solution.py:41
  210.0 22.0 %collective-permute-start.41 = (bf16[480,512]{1,0:T(8,128)(2,1)S(1)}, bf16[480,512]{1,0:T(8,128)(2,1)S(1)}, u32[]{:S(2)}, u32[]{:S(2)}) collective-permute-start(bf16[480,512]{1,0:T(8,128)(2,1)S(1)} %get-tuple-element.137), channel_id=1, source_target_pairs={{0,64},{64,0},{1,65},{65,1},{2,66},{66,2},{3,67},{67,3},{4,68},{68... | collective-permute-start | bytes 1474568 | tf_op jit(solution)/shard_map/ppermute | solution.py:41
  (53 other events, 393.5 us)
Sparse Core Ops, SparseCore 0:
  47.4 37.7 all-gather.2
  133.6 38.9 all-gather.4
  175.0 28.4 reduce-scatter.1

commit v3 on v1

--- a/solution.py
+++ b/solution.py
@@ -224,7 +224,7 @@
         ],
         compiler_params=pltpu.CompilerParams(vmem_limit_bytes=48 * MIB),
         cost_estimate=pl.CostEstimate(
-            flops=6 * n * 2048 * 1024 // COST, bytes_accessed=(12 << 20) // COST, transcendentals=0
+            flops=6 * n * 2048 * 1024, bytes_accessed=12 << 20, transcendentals=0
         ),
         name="weight_grads",
     )(pos, *pieces, *col_pieces)

time: 240 us -> 240 us (level)
    unnamed x80 -> x82, local copies, waits for them, and re-layouts: 17.2 us -> 18.2 us
where the time goes in v3:
time: 240 us; the launch traced here: 239 us
  waiting for transfers between devices  73.7 us (31%)
  Pallas kernels  67.7 us (28%)
  starting transfers between devices  48.4 us (20%)
  local copies, waits for them, and re-layouts  23.9 us (10%)
  between operations  14.5 us (6%)
  other arithmetic  10.8 us (4%)
    ppermute x11, waiting for transfers between devices, send_x(): return lax.ppermute(a, 'x', ring(4, step))  27.6 us
    pallas_call x4, Pallas kernels, weights_call(): pl.pallas_call(functools.partial(weights_kernel, n, places), in_specs=[pl...  27.3 us
    pallas_call x2, Pallas kernels, hidden_call(): pl.pallas_call(functools.partial(hidden_kernel, places, outs), grid=(N_TI...  26.2 us
    ppermute x21, waiting for transfers between devices, swap(): return lax.ppermute(a, axis, [(0, 1), (1, 0)])  24.1 us
    ppermute x10, waiting for transfers between devices, send_z(): return lax.ppermute(a, 'z', ring(4, step))  19.9 us
    ppermute x11, starting transfers between devices, send_x(): return lax.ppermute(a, 'x', ring(4, step))  18.5 us
    unnamed x82, local copies, waits for them, and re-layouts  18.2 us
    ppermute x21, starting transfers between devices, swap(): return lax.ppermute(a, axis, [(0, 1), (1, 0)])  15.2 us
  transfers between devices with their start and end apart: 44, of which 19 were waited for; matrix products, arithmetic and copies ran while one was open for 5% of the time, Pallas kernels for 25%

profile of v3, /device:TPU:0, one launch (start us, length us, event | category | flops | bytes accessed | tf_op | source)
XLA Modules:
  0.0 239.0 jit_solution(4279231859469193244)
XLA Ops:
  18.6 2.8 %collective-permute-done.3 = bf16[2,32,1024]{2,1,0:T(8,128)(2,1)S(1)} collective-permute-done((bf16[2,32,1024]{2,1,0:T(8,128)(2,1)S(1)}, bf16[2,32,1024]{2,1,0:T(8,128)(2,1)S(1)}, u32[]{:S(2)}, u32[]{:S(2)}) %collective-permute-start.3) | collective-permute-done | bytes 131104 | tf_op jit(solution)/shard_map/ppermute | solution.py:33
  23.4 4.5 %collective-permute-done.5 = bf16[2,32,1024]{2,1,0:T(8,128)(2,1)S(1)} collective-permute-done((bf16[2,32,1024]{2,1,0:T(8,128)(2,1)S(1)}, bf16[2,32,1024]{2,1,0:T(8,128)(2,1)S(1)}, u32[]{:S(2)}, u32[]{:S(2)}) %collective-permute-start.5) | collective-permute-done | bytes 131104 | tf_op jit(solution)/shard_map/ppermute | solution.py:33
  29.9 2.5 %collective-permute-start.11 = (bf16[2,32,4096]{2,1,0:T(8,128)(2,1)S(1)}, bf16[2,32,4096]{2,1,0:T(8,128)(2,1)S(1)}, u32[]{:S(2)}, u32[]{:S(2)}) collective-permute-start(bf16[2,32,4096]{2,1,0:T(8,128)(2,1)S(1)} %collective-permute-done.2.refs_3_), channel_id=1, source_target_pairs={{0,6},{2,0},{4,2},{6,4},{1,7},{3,1},{5,3},{7,5},{8,14},{10,8},{12,... | collective-permute-start | bytes 1572872 | tf_op jit(solution)/shard_map/ppermute | solution.py:37
  32.4 13.2 %hidden_grads.2 = (bf16[2784,256]{1,0:T(8,128)(2,1)}, bf16[2,256,924]{2,1,0:T(8,128)(2,1)S(1)}) custom-call(bf16[2,32,4096]{2,1,0:T(8,128)(2,1)S(1)} %pad_maximum_fusion.refs_0_, bf16[2,32,4096]{2,1,0:T(8,128)(2,1)S(1)} %collective-permute-done.1.refs_1_, bf16[2,32,4096]{2,1,0:T(8,128)(2,1)S(1)} %collective-permute-done.refs_2_, ...), custom_call_target="tpu_custom_call" | custom-call | flops 726663168 | bytes 2838528 | tf_op jit(solution)/shard_map/hidden_grads/pallas_call | solution.py:104
  50.4 11.1 %collective-permute-done.14.refs_1_ = bf16[2,32,4096]{2,1,0:T(8,128)(2,1)S(1)} collective-permute-done((bf16[2,32,4096]{2,1,0:T(8,128)(2,1)S(1)}, bf16[2,32,4096]{2,1,0:T(8,128)(2,1)S(1)}, u32[]{:S(2)}, u32[]{:S(2)}) %collective-permute-start.14) | collective-permute-done | bytes 524320 | tf_op jit(solution)/shard_map/ppermute | solution.py:37
  61.5 2.5 %collective-permute-done.13.refs_0_ = bf16[2,32,4096]{2,1,0:T(8,128)(2,1)S(1)} collective-permute-done((bf16[2,32,4096]{2,1,0:T(8,128)(2,1)S(1)}, bf16[2,32,4096]{2,1,0:T(8,128)(2,1)S(1)}, u32[]{:S(2)}, u32[]{:S(2)}) %collective-permute-start.13) | collective-permute-done | bytes 524320 | tf_op jit(solution)/shard_map/ppermute | solution.py:37
  66.0 3.2 %collective-permute-start.21 = (bf16[2,2,4,32,1024]{4,3,2,1,0:T(8,128)(2,1)}, bf16[2,2,4,32,1024]{4,3,2,1,0:T(8,128)(2,1)S(1)}, u32[]{:S(2)}, u32[]{:S(2)}) collective-permute-start(bf16[2,2,4,32,1024]{4,3,2,1,0:T(8,128)(2,1)} %pad_maximum_fusion.1.refs_5_), channel_id=1, source_target_pairs={{0,6},{2,0},{4,2},{6,4},{1,7},{3,1},{5,3},{7,5},{8,14},{10,8},{12,... | collective-permute-start | bytes 3145736 | tf_op jit(solution)/shard_map/ppermute | solution.py:37
  69.2 13.0 %hidden_grads.3 = (bf16[1536,256]{1,0:T(8,128)(2,1)S(1)}, bf16[1248,256]{1,0:T(8,128)(2,1)S(1)}, bf16[2,256,924]{2,1,0:T(8,128)(2,1)}) custom-call(bf16[2,32,4096]{2,1,0:T(8,128)(2,1)S(1)} %collective-permute-done.13.refs_0_, bf16[2,32,4096]{2,1,0:T(8,128)(2,1)S(1)} %collective-permute-done.14.refs_1_, bf16[2,32,4096]{2,1,0:T(8,128)(2,1)S(1)} %copy-done.11, ...), custom_call_target="tpu_custom_call" | custom-call | flops 726663168 | bytes 2838528 | tf_op jit(solution)/shard_map/hidden_grads/pallas_call | solution.py:104
  83.4 2.9 %collective-permute-start.24 = (bf16[1536,256]{1,0:T(8,128)(2,1)S(1)}, bf16[1536,256]{1,0:T(8,128)(2,1)}, u32[]{:S(2)}, u32[]{:S(2)}) collective-permute-start(bf16[1536,256]{1,0:T(8,128)(2,1)S(1)} %get-tuple-element.114.refs_1_), channel_id=1, source_target_pairs={{0,48},{16,0},{32,16},{48,32},{1,49},{17,1},{33,17},{49,33},{2,50}... | collective-permute-start | bytes 2359304 | tf_op jit(solution)/shard_map/ppermute | solution.py:33
  86.3 6.3 %collective-permute-done.19.refs_9_ = bf16[2,2,4,32,1024]{4,3,2,1,0:T(8,128)(2,1)S(1)} collective-permute-done((bf16[2,2,4,32,1024]{4,3,2,1,0:T(8,128)(2,1)}, bf16[2,2,4,32,1024]{4,3,2,1,0:T(8,128)(2,1)S(1)}, u32[]{:S(2)}, u32[]{:S(2)}) %collective-permute-start.19) | collective-permute-done | bytes 1048608 | tf_op jit(solution)/shard_map/ppermute | solution.py:37
  94.7 2.4 collective-permute-start.22
  99.7 14.1 %in_grads_terms.1 = (bf16[4,2,32,4096]{3,2,1,0:T(8,128)(2,1)S(1)}, bf16[4,2,32,4096]{3,2,1,0:T(8,128)(2,1)}) custom-call(s32[3]{0:T(128)S(1)} %pad_add_fusion.pos_ref, bf16[2,256,924]{2,1,0:T(8,128)(2,1)S(1)} %copy-done.13, bf16[2,256,924]{2,1,0:T(8,128)(2,1)S(1)} %copy-done.14, bf16[924,4096]{1,0:T(8,128)(2,1)} %bitcast.36, bf16[924,4096]{1,0:T(8,128)(2,1)} %bitcast.39), custom_call_target="tpu_custom_call" | custom-call | flops 968884224 | bytes 1892352 | tf_op jit(solution)/shard_map/in_grads_terms/pallas_call | solution.py:146
  115.2 6.1 %collective-permute-done.23.refs_2_ = bf16[1536,256]{1,0:T(8,128)(2,1)S(1)} collective-permute-done((bf16[1536,256]{1,0:T(8,128)(2,1)S(1)}, bf16[1536,256]{1,0:T(8,128)(2,1)S(1)}, u32[]{:S(2)}, u32[]{:S(2)}) %collective-permute-start.23) | collective-permute-done | bytes 786464 | tf_op jit(solution)/shard_map/ppermute | solution.py:33
  128.4 8.4 %collective-permute-done.26.refs_4_ = bf16[768,256]{1,0:T(8,128)(2,1)S(1)} collective-permute-done((bf16[768,256]{1,0:T(8,128)(2,1)S(1)}, bf16[768,256]{1,0:T(8,128)(2,1)S(1)}, u32[]{:S(2)}, u32[]{:S(2)}) %collective-permute-start.26) | collective-permute-done | bytes 393248 | tf_op jit(solution)/shard_map/ppermute | solution.py:33
  141.6 7.1 %weight_grads.4 = (bf16[768,512]{1,0:T(8,128)(2,1)S(1)}, bf16[768,512]{1,0:T(8,128)(2,1)S(1)}) custom-call(s32[3]{0:T(128)S(1)} %pad_add_fusion.pos_ref, bf16[11136,256]{1,0:T(8,128)(2,1)} %all-gather.2.cloned.1.call-done.refs_0_, bf16[1536,256]{1,0:T(8,128)(2,1)S(1)} %copy-done.3, bf16[1536,256]{1,0:T(8,128)(2,1)S(1)} %collective-permute-done.23.refs_2_, ...), custom_call_target="tpu_custom_call" | custom-call | flops 3221225472 | bytes 12582912 | tf_op jit(solution)/shard_map/weight_grads/pallas_call | solution.py:215
  154.4 3.0 %collective-permute-start.38 = (bf16[768,512]{1,0:T(8,128)(2,1)}, bf16[768,512]{1,0:T(8,128)(2,1)}, u32[]{:S(2)}, u32[]{:S(2)}) collective-permute-start(bf16[768,512]{1,0:T(8,128)(2,1)} %copy-done.26), channel_id=1, source_target_pairs={{0,64},{64,0},{1,65},{65,1},{2,66},{66,2},{3,67},{67,3},{4,68},{68... | collective-permute-start | bytes 2359304 | tf_op jit(solution)/shard_map/ppermute | solution.py:41
  159.6 7.5 %weight_grads.5 = (bf16[768,512]{1,0:T(8,128)(2,1)S(1)}, bf16[768,512]{1,0:T(8,128)(2,1)S(1)}) custom-call(s32[3]{0:T(128)S(1)} %pad_add_fusion.pos_ref, bf16[11136,256]{1,0:T(8,128)(2,1)} %all-gather.2.cloned.1.call-done.refs_0_, bf16[1536,256]{1,0:T(8,128)(2,1)S(1)} %copy-done.4, bf16[1536,256]{1,0:T(8,128)(2,1)S(1)} %collective-permute-done.23.refs_2_, ...), custom_call_target="tpu_custom_call" | custom-call | flops 3221225472 | bytes 12582912 | tf_op jit(solution)/shard_map/weight_grads/pallas_call | solution.py:215
  174.1 3.0 %collective-permute-start.39 = (bf16[768,512]{1,0:T(8,128)(2,1)}, bf16[768,512]{1,0:T(8,128)(2,1)S(1)}, u32[]{:S(2)}, u32[]{:S(2)}) collective-permute-start(bf16[768,512]{1,0:T(8,128)(2,1)} %copy-done.25), channel_id=1, source_target_pairs={{0,64},{64,0},{1,65},{65,1},{2,66},{66,2},{3,67},{67,3},{4,68},{68... | collective-permute-start | bytes 2359304 | tf_op jit(solution)/shard_map/ppermute | solution.py:41
  186.2 7.0 %weight_grads.6 = (bf16[768,512]{1,0:T(8,128)(2,1)S(1)}, bf16[768,512]{1,0:T(8,128)(2,1)S(1)}) custom-call(s32[3]{0:T(128)S(1)} %pad_add_fusion.pos_ref, bf16[11136,256]{1,0:T(8,128)(2,1)} %all-gather.2.cloned.1.call-done.refs_0_, bf16[1248,256]{1,0:T(8,128)(2,1)S(1)} %copy-done.6, bf16[1248,256]{1,0:T(8,128)(2,1)S(1)} %collective-permute-done.34.refs_2_, ...), custom_call_target="tpu_custom_call" | custom-call | flops 3221225472 | bytes 12582912 | tf_op jit(solution)/shard_map/weight_grads/pallas_call | solution.py:215
  193.2 3.1 %collective-permute-start.40 = (bf16[768,512]{1,0:T(8,128)(2,1)S(1)}, bf16[768,512]{1,0:T(8,128)(2,1)S(1)}, u32[]{:S(2)}, u32[]{:S(2)}) collective-permute-start(bf16[768,512]{1,0:T(8,128)(2,1)S(1)} %get-tuple-element.125), channel_id=1, source_target_pairs={{0,64},{64,0},{1,65},{65,1},{2,66},{66,2},{3,67},{67,3},{4,68},{68... | collective-permute-start | bytes 2359304 | tf_op jit(solution)/shard_map/ppermute | solution.py:41
  198.6 5.7 %weight_grads.7 = (bf16[480,512]{1,0:T(8,128)(2,1)S(1)}, bf16[480,512]{1,0:T(8,128)(2,1)S(1)}) custom-call(s32[3]{0:T(128)S(1)} %pad_add_fusion.pos_ref, bf16[11136,256]{1,0:T(8,128)(2,1)} %all-gather.2.cloned.1.call-done.refs_0_, bf16[1248,256]{1,0:T(8,128)(2,1)S(1)} %copy-done.7, bf16[1248,256]{1,0:T(8,128)(2,1)S(1)} %collective-permute-done.34.refs_2_, ...), custom_call_target="tpu_custom_call" | custom-call | flops 2013265920 | bytes 12582912 | tf_op jit(solution)/shard_map/weight_grads/pallas_call | solution.py:215
  205.3 10.0 %collective-permute-done.40 = bf16[768,512]{1,0:T(8,128)(2,1)S(1)} collective-permute-done((bf16[768,512]{1,0:T(8,128)(2,1)S(1)}, bf16[768,512]{1,0:T(8,128)(2,1)S(1)}, u32[]{:S(2)}, u32[]{:S(2)}) %collective-permute-start.40) | collective-permute-done | bytes 786464 | tf_op jit(solution)/shard_map/ppermute | solution.py:41
  215.6 8.2 %collective-permute-done.41 = bf16[480,512]{1,0:T(8,128)(2,1)S(1)} collective-permute-done((bf16[480,512]{1,0:T(8,128)(2,1)S(1)}, bf16[480,512]{1,0:T(8,128)(2,1)S(1)}, u32[]{:S(2)}, u32[]{:S(2)}) %collective-permute-start.41) | collective-permute-done | bytes 491552 | tf_op jit(solution)/shard_map/ppermute | solution.py:41
  228.9 2.5 %collective-permute-done.33 = bf16[32,4096]{1,0:T(8,128)(2,1)S(1)} collective-permute-done((bf16[32,4096]{1,0:T(8,128)(2,1)S(1)}, bf16[32,4096]{1,0:T(8,128)(2,1)S(1)}, u32[]{:S(2)}, u32[]{:S(2)}) %collective-permute-start.33) | collective-permute-done | bytes 262176 | tf_op jit(solution)/shard_map/ppermute | solution.py:41
  (190 shorter events, 74.2 us)
Async XLA Ops:
  7.2 116.3 %all-gather.2.cloned.1.call-start = ((), (), s32[]{:S(2)}) async-start(), calls=%async_computation.1 | async-start | bytes 7127040 | tf_op jit(solution)/shard_map/all_gather | solution.py:265
  8.4 19.6 %collective-permute-start = (bf16[2,32,4096]{2,1,0:T(8,128)(2,1)S(1)}, bf16[2,32,4096]{2,1,0:T(8,128)(2,1)S(1)}, u32[]{:S(2)}, u32[]{:S(2)}) collective-permute-start(bf16[2,32,4096]{2,1,0:T(8,128)(2,1)S(1)} %pad_maximum_fusion.refs_0_), channel_id=1, source_target_pairs={{0,2},{2,4},{4,6},{6,0},{1,3},{3,5},{5,7},{7,1},{8,10},{10,12},{12... | collective-permute-start | bytes 1572872 | tf_op jit(solution)/shard_map/ppermute | solution.py:37
  10.4 17.5 %collective-permute-start.1 = (bf16[2,32,4096]{2,1,0:T(8,128)(2,1)S(1)}, bf16[2,32,4096]{2,1,0:T(8,128)(2,1)S(1)}, u32[]{:S(2)}, u32[]{:S(2)}) collective-permute-start(bf16[2,32,4096]{2,1,0:T(8,128)(2,1)S(1)} %pad_maximum_fusion.refs_0_), channel_id=1, source_target_pairs={{0,6},{2,0},{4,2},{6,4},{1,7},{3,1},{5,3},{7,5},{8,14},{10,8},{12,... | collective-permute-start | bytes 1572872 | tf_op jit(solution)/shard_map/ppermute | solution.py:37
  12.6 15.3 %collective-permute-start.2 = (bf16[2,32,4096]{2,1,0:T(8,128)(2,1)S(1)}, bf16[2,32,4096]{2,1,0:T(8,128)(2,1)S(1)}, u32[]{:S(2)}, u32[]{:S(2)}) collective-permute-start(bf16[2,32,4096]{2,1,0:T(8,128)(2,1)S(1)} %pad_maximum_fusion.refs_0_), channel_id=1, source_target_pairs={{0,8},{8,0},{1,9},{9,1},{2,10},{10,2},{3,11},{11,3},{4,12},{12,4},... | collective-permute-start | bytes 1572872 | tf_op jit(solution)/shard_map/ppermute | solution.py:41
  28.5 18.1 %collective-permute-start.10 = (bf16[2,32,4096]{2,1,0:T(8,128)(2,1)S(1)}, bf16[2,32,4096]{2,1,0:T(8,128)(2,1)S(1)}, u32[]{:S(2)}, u32[]{:S(2)}) collective-permute-start(bf16[2,32,4096]{2,1,0:T(8,128)(2,1)S(1)} %collective-permute-done.2.refs_3_), channel_id=1, source_target_pairs={{0,2},{2,4},{4,6},{6,0},{1,3},{3,5},{5,7},{7,1},{8,10},{10,12},{12... | collective-permute-start | bytes 1572872 | tf_op jit(solution)/shard_map/ppermute | solution.py:37
  28.7 17.9 %collective-permute-start.12 = (bf16[2,4,32,1024]{3,2,1,0:T(8,128)(2,1)S(1)}, bf16[2,4,32,1024]{3,2,1,0:T(8,128)(2,1)S(1)}, u32[]{:S(2)}, u32[]{:S(2)}) collective-permute-start(bf16[2,4,32,1024]{3,2,1,0:T(8,128)(2,1)S(1)} %pad_maximum_fusion.3), channel_id=1, source_target_pairs={{0,8},{8,0},{1,9},{9,1},{2,10},{10,2},{3,11},{11,3},{4,12},{12,4},... | collective-permute-start | bytes 1572872 | tf_op jit(solution)/shard_map/ppermute | solution.py:41
  29.9 16.7 %collective-permute-start.11 = (bf16[2,32,4096]{2,1,0:T(8,128)(2,1)S(1)}, bf16[2,32,4096]{2,1,0:T(8,128)(2,1)S(1)}, u32[]{:S(2)}, u32[]{:S(2)}) collective-permute-start(bf16[2,32,4096]{2,1,0:T(8,128)(2,1)S(1)} %collective-permute-done.2.refs_3_), channel_id=1, source_target_pairs={{0,6},{2,0},{4,2},{6,4},{1,7},{3,1},{5,3},{7,5},{8,14},{10,8},{12,... | collective-permute-start | bytes 1572872 | tf_op jit(solution)/shard_map/ppermute | solution.py:37
  47.5 176.5 %reduce-scatter.2.cloned.1.call-start = ((), (), s32[]{:S(2)}) async-start(), calls=%async_computation.2 | async-start | bytes 2621440 | tf_op jit(solution)/shard_map/reduce_scatter | solution.py:306
  66.0 26.6 %collective-permute-start.19 = (bf16[2,2,4,32,1024]{4,3,2,1,0:T(8,128)(2,1)}, bf16[2,2,4,32,1024]{4,3,2,1,0:T(8,128)(2,1)S(1)}, u32[]{:S(2)}, u32[]{:S(2)}) collective-permute-start(bf16[2,2,4,32,1024]{4,3,2,1,0:T(8,128)(2,1)} %pad_maximum_fusion.1.refs_5_), channel_id=1, source_target_pairs={{0,2},{2,4},{4,6},{6,0},{1,3},{3,5},{5,7},{7,1},{8,10},{10,12},{12... | collective-permute-start | bytes 3145736 | tf_op jit(solution)/shard_map/ppermute | solution.py:37
  66.0 26.7 %collective-permute-start.21 = (bf16[2,2,4,32,1024]{4,3,2,1,0:T(8,128)(2,1)}, bf16[2,2,4,32,1024]{4,3,2,1,0:T(8,128)(2,1)S(1)}, u32[]{:S(2)}, u32[]{:S(2)}) collective-permute-start(bf16[2,2,4,32,1024]{4,3,2,1,0:T(8,128)(2,1)} %pad_maximum_fusion.1.refs_5_), channel_id=1, source_target_pairs={{0,6},{2,0},{4,2},{6,4},{1,7},{3,1},{5,3},{7,5},{8,14},{10,8},{12,... | collective-permute-start | bytes 3145736 | tf_op jit(solution)/shard_map/ppermute | solution.py:37
  69.2 52.1 %collective-permute-start.25 = (bf16[2,2,4,32,1024]{4,3,2,1,0:T(8,128)(2,1)}, bf16[2,2,4,32,1024]{4,3,2,1,0:T(8,128)(2,1)}, u32[]{:S(2)}, u32[]{:S(2)}) collective-permute-start(bf16[2,2,4,32,1024]{4,3,2,1,0:T(8,128)(2,1)} %pad_maximum_fusion.1.refs_5_), channel_id=1, source_target_pairs={{0,1},{1,0},{2,3},{3,2},{4,5},{5,4},{6,7},{7,6},{8,9},{9,8},{10,11... | collective-permute-start | bytes 3145736 | tf_op jit(solution)/shard_map/ppermute | solution.py:41
  83.1 38.3 %collective-permute-start.23 = (bf16[1536,256]{1,0:T(8,128)(2,1)S(1)}, bf16[1536,256]{1,0:T(8,128)(2,1)S(1)}, u32[]{:S(2)}, u32[]{:S(2)}) collective-permute-start(bf16[1536,256]{1,0:T(8,128)(2,1)S(1)} %get-tuple-element.114.refs_1_), channel_id=1, source_target_pairs={{0,16},{16,32},{32,48},{48,0},{1,17},{17,33},{33,49},{49,1},{2,18}... | collective-permute-start | bytes 2359304 | tf_op jit(solution)/shard_map/ppermute | solution.py:33
  83.4 37.9 %collective-permute-start.24 = (bf16[1536,256]{1,0:T(8,128)(2,1)S(1)}, bf16[1536,256]{1,0:T(8,128)(2,1)}, u32[]{:S(2)}, u32[]{:S(2)}) collective-permute-start(bf16[1536,256]{1,0:T(8,128)(2,1)S(1)} %get-tuple-element.114.refs_1_), channel_id=1, source_target_pairs={{0,48},{16,0},{32,16},{48,32},{1,49},{17,1},{33,17},{49,33},{2,50}... | collective-permute-start | bytes 2359304 | tf_op jit(solution)/shard_map/ppermute | solution.py:33
  92.6 28.7 %collective-permute-start.20 = (bf16[2,4,32,1024]{3,2,1,0:T(8,128)(2,1)S(1)}, bf16[2,4,32,1024]{3,2,1,0:T(8,128)(2,1)S(1)}, u32[]{:S(2)}, u32[]{:S(2)}) collective-permute-start(bf16[2,4,32,1024]{3,2,1,0:T(8,128)(2,1)S(1)} %slice_bitcast_fusion.1), channel_id=1, source_target_pairs={{0,2},{2,4},{4,6},{6,0},{1,3},{3,5},{5,7},{7,1},{8,10},{10,12},{12... | collective-permute-start | bytes 1572872 | tf_op jit(solution)/shard_map/ppermute | solution.py:37
  94.7 26.6 %collective-permute-start.22 = (bf16[2,4,32,1024]{3,2,1,0:T(8,128)(2,1)}, bf16[2,4,32,1024]{3,2,1,0:T(8,128)(2,1)S(1)}, u32[]{:S(2)}, u32[]{:S(2)}) collective-permute-start(bf16[2,4,32,1024]{3,2,1,0:T(8,128)(2,1)} %slice_bitcast_fusion), channel_id=1, source_target_pairs={{0,6},{2,0},{4,2},{6,4},{1,7},{3,1},{5,3},{7,5},{8,14},{10,8},{12,... | collective-permute-start | bytes 1572872 | tf_op jit(solution)/shard_map/ppermute | solution.py:37
  123.5 16.8 %collective-permute-start.28 = (bf16[4,2,32,4096]{3,2,1,0:T(8,128)(2,1)}, bf16[4,2,32,4096]{3,2,1,0:T(8,128)(2,1)S(1)}, u32[]{:S(2)}, u32[]{:S(2)}) collective-permute-start(bf16[4,2,32,4096]{3,2,1,0:T(8,128)(2,1)} %get-tuple-element.102), channel_id=1, source_target_pairs={{0,1},{1,0},{2,3},{3,2},{4,5},{5,4},{6,7},{7,6},{8,9},{9,8},{10,11... | collective-permute-start | bytes 6291464 | tf_op jit(solution)/shard_map/ppermute | solution.py:41
  123.5 16.7 %collective-permute-start.29 = (bf16[2,2,4,32,1024]{4,3,2,1,0:T(8,128)(2,1)}, bf16[2,2,4,32,1024]{4,3,2,1,0:T(8,128)(2,1)S(1)}, u32[]{:S(2)}, u32[]{:S(2)}) collective-permute-start(bf16[2,2,4,32,1024]{4,3,2,1,0:T(8,128)(2,1)} %copy-done.28), channel_id=1, source_target_pairs={{0,1},{1,0},{2,3},{3,2},{4,5},{5,4},{6,7},{7,6},{8,9},{9,8},{10,11... | collective-permute-start | bytes 3145736 | tf_op jit(solution)/shard_map/ppermute | solution.py:41
  124.0 16.2 %collective-permute-start.32 = (bf16[2,2,4,32,1024]{4,3,2,1,0:T(8,128)(2,1)}, bf16[2,2,4,32,1024]{4,3,2,1,0:T(8,128)(2,1)S(1)}, u32[]{:S(2)}, u32[]{:S(2)}) collective-permute-start(bf16[2,2,4,32,1024]{4,3,2,1,0:T(8,128)(2,1)} %copy-done.27), channel_id=1, source_target_pairs={{0,1},{1,0},{2,3},{3,2},{4,5},{5,4},{6,7},{7,6},{8,9},{9,8},{10,11... | collective-permute-start | bytes 3145736 | tf_op jit(solution)/shard_map/ppermute | solution.py:41
  151.0 18.3 %collective-permute-start.34 = (bf16[1248,256]{1,0:T(8,128)(2,1)}, bf16[1248,256]{1,0:T(8,128)(2,1)S(1)}, u32[]{:S(2)}, u32[]{:S(2)}) collective-permute-start(bf16[1248,256]{1,0:T(8,128)(2,1)} %copy-done.5), channel_id=1, source_target_pairs={{0,16},{16,32},{32,48},{48,0},{1,17},{17,33},{33,49},{49,1},{2,18}... | collective-permute-start | bytes 1916936 | tf_op jit(solution)/shard_map/ppermute | solution.py:33
  152.2 17.1 %collective-permute-start.35 = (bf16[1248,256]{1,0:T(8,128)(2,1)}, bf16[1248,256]{1,0:T(8,128)(2,1)S(1)}, u32[]{:S(2)}, u32[]{:S(2)}) collective-permute-start(bf16[1248,256]{1,0:T(8,128)(2,1)} %copy-done.5), channel_id=1, source_target_pairs={{0,48},{16,0},{32,16},{48,32},{1,49},{17,1},{33,17},{49,33},{2,50}... | collective-permute-start | bytes 1916936 | tf_op jit(solution)/shard_map/ppermute | solution.py:33
  154.4 22.6 %collective-permute-start.38 = (bf16[768,512]{1,0:T(8,128)(2,1)}, bf16[768,512]{1,0:T(8,128)(2,1)}, u32[]{:S(2)}, u32[]{:S(2)}) collective-permute-start(bf16[768,512]{1,0:T(8,128)(2,1)} %copy-done.26), channel_id=1, source_target_pairs={{0,64},{64,0},{1,65},{65,1},{2,66},{66,2},{3,67},{67,3},{4,68},{68... | collective-permute-start | bytes 2359304 | tf_op jit(solution)/shard_map/ppermute | solution.py:41
  174.1 24.6 %collective-permute-start.39 = (bf16[768,512]{1,0:T(8,128)(2,1)}, bf16[768,512]{1,0:T(8,128)(2,1)S(1)}, u32[]{:S(2)}, u32[]{:S(2)}) collective-permute-start(bf16[768,512]{1,0:T(8,128)(2,1)} %copy-done.25), channel_id=1, source_target_pairs={{0,64},{64,0},{1,65},{65,1},{2,66},{66,2},{3,67},{67,3},{4,68},{68... | collective-permute-start | bytes 2359304 | tf_op jit(solution)/shard_map/ppermute | solution.py:41
  193.2 22.1 %collective-permute-start.40 = (bf16[768,512]{1,0:T(8,128)(2,1)S(1)}, bf16[768,512]{1,0:T(8,128)(2,1)S(1)}, u32[]{:S(2)}, u32[]{:S(2)}) collective-permute-start(bf16[768,512]{1,0:T(8,128)(2,1)S(1)} %get-tuple-element.125), channel_id=1, source_target_pairs={{0,64},{64,0},{1,65},{65,1},{2,66},{66,2},{3,67},{67,3},{4,68},{68... | collective-permute-start | bytes 2359304 | tf_op jit(solution)/shard_map/ppermute | solution.py:41
  204.4 19.3 %collective-permute-start.41 = (bf16[480,512]{1,0:T(8,128)(2,1)S(1)}, bf16[480,512]{1,0:T(8,128)(2,1)S(1)}, u32[]{:S(2)}, u32[]{:S(2)}) collective-permute-start(bf16[480,512]{1,0:T(8,128)(2,1)S(1)} %get-tuple-element.131), channel_id=1, source_target_pairs={{0,64},{64,0},{1,65},{65,1},{2,66},{66,2},{3,67},{67,3},{4,68},{68... | collective-permute-start | bytes 1474568 | tf_op jit(solution)/shard_map/ppermute | solution.py:41
  (61 other events, 386.0 us)
Sparse Core Ops, SparseCore 0:
  47.6 75.8 all-gather.1
  151.1 31.5 reduce-scatter.1
